TPU v7x, 32 devices: a whole 2x2x4 slice. The times are simulated.
32 devices in a mesh: head: 4 (over y, core), seq: 8 (over z, x).
Axes of the slice: x: 2, y: 2, z: 4, core: 2. Of those that a mesh axis runs over, the one named last changes fastest.
Arguments:
- queries: bfloat16 [4, 1024, 256], P('head', 'seq'), may hold values from -6 to 6
- key_rows: bfloat16 [4, 1024, 256], P('head', 'seq'), may hold values from -6 to 6
- value_rows: bfloat16 [4, 1024, 256], P('head', 'seq'), may hold values from -6 to 6
- out_grad: bfloat16 [4, 1024, 256], P('head', 'seq'), may hold values from -6 to 6
- step_sizes: float32 [4, 1024], P('head', 'seq'), may hold values from 0.0001 to 0.0004
- norm_gain: float32 [4, 256], P('head'), may hold values from 0.1 to 1.9
- gate_init: bfloat16 [4, 256, 768], P('head', 'seq'), may hold values from -0.90625 to 0.90625
- up_init: bfloat16 [4, 256, 768], P('head', 'seq'), may hold values from -0.90625 to 0.90625
- down_init: bfloat16 [4, 256, 768], P('head', 'seq'), may hold values from -0.90625 to 0.90625
- gate_saved: bfloat16 [4, 256, 768], P('head', 'seq'), may hold values from -0.90625 to 0.90625
- up_saved: bfloat16 [4, 256, 768], P('head', 'seq'), may hold values from -0.90625 to 0.90625
- down_saved: bfloat16 [4, 256, 768], P('head', 'seq'), may hold values from -0.90625 to 0.90625
Outputs:
- grad_queries: bfloat16 [4, 1024, 256], P('head', 'seq')
- grad_keys: bfloat16 [4, 1024, 256], P('head', 'seq')
- grad_values: bfloat16 [4, 1024, 256], P('head', 'seq')
- grad_gate: float32 [4, 256, 768], P('head', 'seq')
- grad_up: float32 [4, 256, 768], P('head', 'seq')
- grad_down: float32 [4, 256, 768], P('head', 'seq')
All inputs are finite; a program needn't handle non-finite values.
Results may differ from a plain program's by a relative error of at most 0.0085.
The roundings to bfloat16 on the way count: a program that leaves them out, or rounds other values in their place, can miss the bound.
Values may be sent and summed in bfloat16 or wider, within the bound.
No kernel may reach another device: no remote copies, remote signals or barrier semaphores. Data moves between devices by JAX's collectives and lax.ppermute only.
A program may use at most 64 MiB of HBM per device.

v0:
```python
import jax
import jax.numpy as jnp
from jax import lax
from jax.sharding import PartitionSpec as P

HEADS = 4
HD = 256


def silu_parts(pre_act):
    sigmoid_val = jax.nn.sigmoid(pre_act)
    silu_val = pre_act * sigmoid_val
    silu_slope = sigmoid_val * (1.0 + pre_act * (1.0 - sigmoid_val))
    silu_bend = sigmoid_val * (1.0 - sigmoid_val) * (2.0 + pre_act * (1.0 - 2.0 * sigmoid_val))
    return (silu_val, silu_slope, silu_bend)


def matmul_f32(left_op, right_op):
    return jnp.dot(left_op, right_op, preferred_element_type=jnp.float32)


def matmul_nt(left_op, right_op):
    return jnp.einsum("th,dh->td", left_op, right_op, preferred_element_type=jnp.float32)


def outer_sum(left_op, right_op):
    return jnp.einsum("td,th->dh", left_op, right_op, preferred_element_type=jnp.float32)


def column_sq(weight):
    return jnp.sum(jnp.square(weight.astype(jnp.float32)), axis=0)


def local(
    queries,
    key_rows,
    value_rows,
    out_grad,
    step_sizes,
    norm_gain,
    gate_init,
    up_init,
    down_init,
    gate_saved,
    up_saved,
    down_saved,
):
    hidden_n = gate_init.shape[2]
    slab_rows = gate_init.shape[1]
    query_tok = queries[0]
    key_tok = key_rows[0]
    value_tok = value_rows[0]
    grad_tok = out_grad[0].astype(jnp.float32)
    rates = step_sizes[0]
    gains = norm_gain[0]
    init_slab = jnp.concatenate((gate_init[0], up_init[0], down_init[0]), axis=1)
    saved_slab = jnp.concatenate((gate_saved[0], up_saved[0], down_saved[0]), axis=1)
    init_full, saved_full = (
        lax.all_gather(init_slab, "seq", axis=0, tiled=True),
        lax.all_gather(saved_slab, "seq", axis=0, tiled=True),
    )
    norm_init = jnp.sqrt(column_sq(init_full) + 1e-06)
    norm_saved = jnp.sqrt(column_sq(saved_full) + 1e-06)
    scale_ratio = norm_init / norm_saved
    normed_full = (saved_full.astype(jnp.float32) * scale_ratio).astype(jnp.bfloat16)
    normed_gate = normed_full[:, :hidden_n]
    normed_up = normed_full[:, hidden_n : 2 * hidden_n]
    normed_down = normed_full[:, 2 * hidden_n :]
    q_gate = matmul_f32(query_tok, normed_gate)
    q_up = matmul_f32(query_tok, normed_up)
    gate_act, gate_slope, gate_bend = silu_parts(q_gate)
    q_hidden = (gate_act * q_up).astype(jnp.bfloat16)
    apply_out = matmul_nt(q_hidden, normed_down)
    full_width = HEADS * HD
    square_sum, gain_sum = lax.psum(
        (jnp.sum(jnp.square(apply_out), axis=1), jnp.sum(apply_out * gains * grad_tok, axis=1)),
        "head",
    )
    root = jnp.sqrt(square_sum / full_width + 1e-05)[:, None]
    gain_dot = (gain_sum / full_width)[:, None]
    out_delta = (gains * grad_tok / root - apply_out * gain_dot / root**3).astype(jnp.bfloat16)
    delta_hidden = matmul_f32(out_delta, normed_down)
    delta_gate = (delta_hidden * q_up * gate_slope).astype(jnp.bfloat16)
    delta_up = (delta_hidden * gate_act).astype(jnp.bfloat16)
    grad_q = (matmul_nt(delta_gate, normed_gate) + matmul_nt(delta_up, normed_up)).astype(
        jnp.bfloat16
    )
    apply_local = jnp.concatenate(
        (
            outer_sum(query_tok, delta_gate),
            outer_sum(query_tok, delta_up),
            outer_sum(out_delta, q_hidden),
        ),
        axis=1,
    )
    apply_full = lax.psum(apply_local, "seq")
    saved_f32 = saved_full.astype(jnp.float32)
    col_dot = jnp.sum(saved_f32 * apply_full, axis=0)
    cot_full = apply_full * scale_ratio - saved_f32 * (col_dot * norm_init / norm_saved**3)
    cot_bf = cot_full.astype(jnp.bfloat16)
    first_row = lax.axis_index("seq") * slab_rows
    cot_slab = lax.dynamic_slice_in_dim(cot_full, first_row, slab_rows, 0)
    direct = cot_slab + init_slab.astype(jnp.float32) * (col_dot / (norm_init * norm_saved))
    init_gate = init_full[:, :hidden_n]
    init_up = init_full[:, hidden_n : 2 * hidden_n]
    init_down = init_full[:, 2 * hidden_n :]
    cot_gate = cot_bf[:, :hidden_n]
    cot_up = cot_bf[:, hidden_n : 2 * hidden_n]
    cot_down = cot_bf[:, 2 * hidden_n :]
    k_gate = matmul_f32(key_tok, init_gate)
    k_up = matmul_f32(key_tok, init_up)
    k_act, k_slope, k_bend = silu_parts(k_gate)
    scaled_values = (rates[:, None] * value_tok.astype(jnp.float32)).astype(jnp.bfloat16)
    k_proj = matmul_f32(scaled_values, init_down)
    k_hidden = (k_act * k_up).astype(jnp.bfloat16)
    rise_gate = (k_proj * k_up * k_slope).astype(jnp.bfloat16)
    rise_up = (k_proj * k_act).astype(jnp.bfloat16)
    back_gate = matmul_f32(key_tok, cot_gate)
    back_up = matmul_f32(key_tok, cot_up)
    back_hidden = matmul_f32(scaled_values, cot_down)
    back_proj = (back_gate * k_up * k_slope + back_up * k_act).astype(jnp.bfloat16)
    back_kup = (back_gate * k_proj * k_slope + back_hidden * k_act).astype(jnp.bfloat16)
    back_kgate = (
        back_gate * k_proj * k_up * k_bend + (back_up * k_proj + back_hidden * k_up) * k_slope
    ).astype(jnp.bfloat16)
    grad_k = (
        matmul_nt(rise_gate, cot_gate)
        + matmul_nt(rise_up, cot_up)
        + matmul_nt(back_kgate, init_gate)
        + matmul_nt(back_kup, init_up)
    ).astype(jnp.bfloat16)
    grad_v = (
        rates[:, None] * (matmul_nt(k_hidden, cot_down) + matmul_nt(back_proj, init_down))
    ).astype(jnp.bfloat16)
    inner_slab = lax.psum_scatter(
        jnp.concatenate(
            (
                outer_sum(key_tok, back_kgate),
                outer_sum(key_tok, back_kup),
                outer_sum(scaled_values, back_proj),
            ),
            axis=1,
        ),
        "seq",
        scatter_dimension=0,
        tiled=True,
    )
    grad_total = direct + inner_slab
    return (
        grad_q[None],
        grad_k[None],
        grad_v[None],
        grad_total[None, :, :hidden_n],
        grad_total[None, :, hidden_n : 2 * hidden_n],
        grad_total[None, :, 2 * hidden_n :],
    )


def solution(mesh):
    return jax.shard_map(
        local,
        mesh=mesh,
        in_specs=(
            P("head", "seq", None),
            P("head", "seq", None),
            P("head", "seq", None),
            P("head", "seq", None),
            P("head", "seq"),
            P("head", None),
            P("head", "seq", None),
            P("head", "seq", None),
            P("head", "seq", None),
            P("head", "seq", None),
            P("head", "seq", None),
            P("head", "seq", None),
        ),
        out_specs=(
            P("head", "seq", None),
            P("head", "seq", None),
            P("head", "seq", None),
            P("head", "seq", None),
            P("head", "seq", None),
            P("head", "seq", None),
        ),
        check_vma=False,
    )
```

profile of v0, /device:TPU:0, one launch (start us, length us, event | category | flops | bytes accessed | tf_op | source)
XLA Modules:
  0.0 310.4 jit_solution(8203015390436726812)
XLA Ops:
  7.2 0.0 all-gather.3.cloned.1.call-start
  7.2 1.5 pad_maximum_fusion.2
  8.8 0.0 all-gather.3.cloned.1.call-update
  8.8 0.0 all-gather.5.cloned.1.call-start
  8.8 1.5 pad_maximum_fusion.3
  10.4 0.0 all-reduce.3.cloned.1.call-start
  10.4 43.6 %all-gather.3.cloned.1.call-done = bf16[256,2304]{1,0:T(8,128)(2,1)} async-done(((bf16[32,2304]{1,0:T(8,128)(2,1)}), bf16[256,2304]{1,0:T(8,128)(2,1)}) %all-gather.3.cloned.1.call-update) | async-done | bytes 1179664 | tf_op jit(solution)/shard_map/all_gather | solution.py:60
  54.0 1.6 copy.37
  55.6 0.4 fusion
  55.9 40.1 %all-gather.5.cloned.1.call-done = bf16[256,2304]{1,0:T(8,128)(2,1)} async-done(((bf16[32,2304]{1,0:T(8,128)(2,1)}), bf16[256,2304]{1,0:T(8,128)(2,1)}) %all-gather.5.cloned.1.call-update) | async-done | bytes 1179664 | tf_op jit(solution)/shard_map/all_gather | solution.py:59
  96.0 1.5 multiply_reduce_fusion
  97.6 0.4 fusion.1
  98.0 0.5 copy-done.14
  98.4 0.3 convolution_bitcast_fusion.9
  98.7 1.0 multiply_convert_fusion.5
  99.7 0.3 fusion.47
  100.1 5.7 %all-reduce = (f32[128]{0:T(128)S(1)}, f32[128]{0:T(128)S(1)}) all-reduce(f32[128]{0:T(128)S(1)} %get-tuple-element.19, f32[128]{0:T(128)S(1)} %get-tuple-element.18), channel_id=1, replica_groups=mesh['head'=4,'seq'=8] {'head'}, use_global_device_ids=true, to_apply=%region_3.0 | all-reduce | flops 256 | bytes 2048 | tf_op jit(solution)/shard_map/psum | solution.py:75
  105.7 0.3 fusion.64
  106.1 0.6 copy-done.23
  106.7 0.1 copy-done.29
  106.8 0.4 multiply_convert_fusion.3
  107.2 0.2 convolution_bitcast_fusion.2
  107.5 0.2 convolution_bitcast_fusion.3
  107.7 1.6 pad_maximum_fusion
  109.4 0.0 reduce-scatter.4.cloned.1.call-start
  109.4 1.2 copy-done.1
  110.6 1.1 convolution_bitcast_fusion.7
  111.7 1.1 convolution_bitcast_fusion.6
  112.7 0.3 fusion.33
  113.1 104.2 %all-reduce.3.cloned.1.call-done = f32[256,2304]{0,1:T(8,128)} async-done(((f32[256,2304]{0,1:T(8,128)}), f32[256,2304]{0,1:T(8,128)}) %all-reduce.3.cloned.1.call-update) | async-done | bytes 2359312 | tf_op jit(solution)/shard_map/psum | solution.py:96
  217.3 2.2 fusion.2
  219.5 0.6 multiply_divide_fusion
  220.1 2.2 fusion.70
  222.3 0.2 convolution_bitcast_fusion.5
  222.6 0.3 fusion.21
  222.9 0.7 copy-done.18
  223.6 0.3 copy-done.20
  223.9 0.5 add_convert_fusion
  224.4 0.3 fusion.60
  224.7 0.2 convolution_bitcast_fusion
  225.0 0.2 convolution_bitcast_fusion.1
  225.3 1.6 pad_maximum_fusion.1
  226.9 3.1 copy.57
  230.0 0.9 copy-done.7
  230.9 0.3 copy.47
  231.2 0.1 copy-done.4
  231.3 0.2 fusion.41
  231.6 0.9 fusion.10
  232.4 0.1 copy-done.6
  232.6 1.6 fusion.26
  234.3 0.3 convolution_add_fusion.3
  234.6 0.6 copy-done.11
  235.2 0.3 convolution_add_fusion.2
  235.5 0.9 fusion.9
  236.4 0.3 fusion.19
  236.7 0.6 copy-done.13
  237.3 0.9 fusion.8
  238.3 59.9 %reduce-scatter.4.cloned.1.call-done = f32[32,2304]{1,0:T(8,128)} async-done(((f32[256,2304]{1,0:T(8,128)}), f32[32,2304]{1,0:T(8,128)}) %reduce-scatter.4.cloned.1.call-update) | async-done | bytes 294928
  298.2 1.3 copy.58
  299.5 2.0 add_add_fusion
  301.5 0.1 slice_bitcast_fusion
  301.6 0.8 copy.49
  302.3 0.8 copy.50
  303.1 0.8 copy.51
  (54 shorter events, 0.2 us)
Async XLA Ops:
  7.2 102.3 %copy-start = (bf16[1,128,256]{2,1,0:T(8,128)(2,1)S(1)}, bf16[1,128,256]{2,1,0:T(8,128)(2,1)}, u32[]{:S(2)}) copy-start(bf16[1,128,256]{2,1,0:T(8,128)(2,1)} %param.13) | copy-start | bytes 196612
  7.2 46.8 %all-gather.3.cloned.1.call-start = ((), (), s32[]{:S(2)}) async-start(), calls=%async_computation.1 | async-start | bytes 1327104 | tf_op jit(solution)/shard_map/all_gather | solution.py:60
  8.8 87.2 %all-gather.5.cloned.1.call-start = ((), (), s32[]{:S(2)}) async-start(), calls=%async_computation.2 | async-start | bytes 1327104 | tf_op jit(solution)/shard_map/all_gather | solution.py:59
  10.4 206.9 %all-reduce.3.cloned.1.call-start = ((), (), s32[]{:S(2)}) async-start(), calls=%async_computation.3 | async-start | bytes 4718592 | tf_op jit(solution)/shard_map/psum | solution.py:96
  97.6 0.8 copy-start.14
  98.4 7.7 %copy-start.3 = (bf16[256,2304]{0,1:T(8,128)(2,1)}, bf16[256,2304]{0,1:T(8,128)(2,1)S(1)}, u32[]{:S(2)}) copy-start(bf16[256,2304]{0,1:T(8,128)(2,1)S(1)} %fusion.1) | copy-start | bytes 3538948
  98.7 1.1 copy-start.22
  98.7 1.0 copy-start.24
  98.7 1.0 copy-start.28
  105.7 1.0 copy-start.23
  105.7 1.1 copy-start.29
  109.3 1.3 copy-start.1
  109.4 3.4 %copy-start.15 = (bf16[1,128,256]{2,1,0:T(8,128)(2,1)S(1)}, bf16[1,128,256]{2,1,0:T(8,128)(2,1)}, u32[]{:S(2)}) copy-start(bf16[1,128,256]{2,1,0:T(8,128)(2,1)} %param.14) | copy-start | bytes 196612
  109.4 3.4 %copy-start.26 = (f32[1,128]{1,0:T(1,128)S(1)}, f32[1,128]{1,0:T(1,128)}, u32[]{:S(2)}) copy-start(f32[1,128]{1,0:T(1,128)} %param.16) | copy-start | bytes 1540
  109.4 188.8 %reduce-scatter.4.cloned.1.call-start = ((), (), s32[]{:S(2)}) async-start(), calls=%async_computation.4 | async-start | bytes 2654208
  113.1 109.8 %copy-start.16 = (f32[128,768]{0,1:T(8,128)}, f32[128,768]{0,1:T(8,128)S(1)}, u32[]{:S(2)}) copy-start(f32[128,768]{0,1:T(8,128)S(1)} %fusion.33) | copy-start | bytes 1179652
  217.3 2.8 copy-start.2
  222.3 2.1 copy-start.5
  222.3 1.3 copy-start.18
  222.3 1.5 copy-start.20
  224.4 0.8 copy-start.8
  224.4 0.8 copy-start.10
  224.4 0.8 copy-start.12
  229.9 0.9 copy-start.7
  229.9 1.4 copy-start.4
  231.3 1.3 copy-start.6
  232.6 1.7 copy-start.17
  232.6 1.7 copy-start.21
  234.2 0.9 copy-start.11
  234.3 1.2 copy-start.9
  235.2 1.2 copy-start.19
  236.4 0.9 copy-start.13
  236.4 0.9 copy-start.27
  237.3 62.2 %copy-start.25 = (f32[2304]{0:T(1024)S(1)}, f32[2304]{0:T(1024)}, u32[]{:S(2)}) copy-start(f32[2304]{0:T(1024)} %get-tuple-element.32) | copy-start | bytes 27652
Sparse Core Ops, SparseCore 0:
  10.2 43.7 all-gather.2
  56.2 39.8 all-gather.4
  109.5 107.7 all-reduce.2
  230.1 68.0 reduce-scatter.3
where the time goes:
time: 311 us; the launch traced here: 310 us
  waiting for transfers between devices  248 us (80%)
  other arithmetic  15.5 us (5%)
  local copies, waits for them, and re-layouts  14.4 us (5%)
  between operations  14.2 us (5%)
  matrix products  12.7 us (4%)
  blocking collectives  5.67 us (2%)
    psum x1, waiting for transfers between devices, local(): apply_full = lax.psum(apply_local, 'seq')  104 us
    unnamed x5, waiting for transfers between devices  60 us
    all_gather x1, waiting for transfers between devices, local(): lax.all_gather(saved_slab, 'seq', axis=0, tiled=True)  43.6 us
    all_gather x1, waiting for transfers between devices, local(): lax.all_gather(init_slab, 'seq', axis=0, tiled=True)  40.1 us
    unnamed x65, local copies, waits for them, and re-layouts  12.4 us
  transfers between devices with their start and end apart: 4, of which 4 were waited for; matrix products, arithmetic and copies ran while one was open for 4% of the time, Pallas kernels for 0%

commit v1 on v0

v1 whole, which is shorter than its diff:
```python
import jax
import jax.numpy as jnp
from jax import lax
from jax.sharding import PartitionSpec as P

EPS_COL = 1e-06
EPS_ROOT = 1e-05
BF = jnp.bfloat16
F32 = jnp.float32


def silu_parts(pre_act):
    sigmoid_val = jax.nn.sigmoid(pre_act)
    silu_val = pre_act * sigmoid_val
    silu_slope = sigmoid_val * (1.0 + pre_act * (1.0 - sigmoid_val))
    silu_bend = sigmoid_val * (1.0 - sigmoid_val) * (2.0 + pre_act * (1.0 - 2.0 * sigmoid_val))
    return (silu_val, silu_slope, silu_bend)


def mm(left_op, right_op):
    return jnp.dot(left_op, right_op, preferred_element_type=F32)


def mm_nt(left_op, right_op):
    return lax.dot_general(left_op, right_op, (((1,), (1,)), ((), ())), preferred_element_type=F32)


def mm_tn(left_op, right_op):
    return lax.dot_general(left_op, right_op, (((0,), (0,)), ((), ())), preferred_element_type=F32)


def column_norm(weight):
    return jnp.sqrt(jnp.sum(jnp.square(weight.astype(F32)), axis=0, keepdims=True) + EPS_COL)


def send(block, axis, size, dist):
    if dist == 0:
        return block
    return lax.ppermute(block, axis, [(i, i ^ dist) for i in range(size)])


def make_local(seq_n, head_n, group):
    def local(q, k, v, og, rates, gains, gi, ui, di, gs, us, ds):
        q, k, v, og, rates = q[0], k[0], v[0], og[0], rates[0]
        hidden = gi.shape[2]
        slab = hidden // group
        rows = gi.shape[1]
        feat = q.shape[1]
        width = head_n * feat
        me = lax.axis_index("seq")
        mine = lax.rem(me, group)
        near = range(group)
        every = range(seq_n)

        sv = (rates[:, None] * v.astype(F32)).astype(BF)
        packed = jnp.stack([w[0].reshape(rows, group, slab) for w in (gs, us, ds, gi, ui, di)], axis=2)
        packed = packed.reshape(rows, group, 6 * slab).transpose(1, 0, 2)
        wsend = [lax.dynamic_index_in_dim(packed, mine ^ d, 0, keepdims=False) for d in near]
        wrecv = [send(wsend[d % group], "seq", seq_n, d) for d in every]
        qs = [send(q, "seq", seq_n, d) for d in near]
        ks = [send(k, "seq", seq_n, d) for d in near]
        vs = [send(sv, "seq", seq_n, d) for d in near]
        qs += [send(q, "seq", seq_n, d) for d in every[group:]]

        wall = jnp.zeros((seq_n * rows, 6 * slab), BF)
        for d in every:
            wall = lax.dynamic_update_slice_in_dim(wall, wrecv[d], (me ^ d) * rows, 0)
        saved = [wall[:, i * slab : (i + 1) * slab] for i in range(3)]
        init = [wall[:, (i + 3) * slab : (i + 4) * slab] for i in range(3)]
        norm_init = [column_norm(w) for w in init]
        norm_saved = [column_norm(w) for w in saved]
        ratio = [norm_init[i] / norm_saved[i] for i in range(3)]
        normed = [(saved[i].astype(F32) * ratio[i]).astype(BF) for i in range(3)]

        qall = jnp.concatenate(qs, axis=0)
        q_gate = mm(qall, normed[0])
        q_up = mm(qall, normed[1])
        act, slope, _ = silu_parts(q_gate)
        q_hidden = (act * q_up).astype(BF)
        own_tok = q.shape[0]
        near_tok = group * own_tok
        part = mm_nt(q_hidden[:near_tok], normed[2]).astype(BF)
        parts = [send(part[d * own_tok : (d + 1) * own_tok], "seq", seq_n, d) for d in near]
        apply_out = sum(p.astype(F32) for p in parts)

        gg = gains * og.astype(F32)
        sums = lax.psum(
            jnp.stack((jnp.sum(apply_out * apply_out, axis=1), jnp.sum(apply_out * gg, axis=1))), "head"
        )
        root = jnp.sqrt(sums[0] / width + EPS_ROOT)[:, None]
        gain_dot = (sums[1] / width)[:, None]
        out_delta = (gg / root - apply_out * gain_dot / root**3).astype(BF)
        odall = jnp.concatenate([send(out_delta, "seq", seq_n, d) for d in every], axis=0)

        delta_hidden = mm(odall, normed[2])
        delta_gate = (delta_hidden * q_up * slope).astype(BF)
        delta_up = (delta_hidden * act).astype(BF)
        gq = (mm_nt(delta_gate[:near_tok], normed[0]) + mm_nt(delta_up[:near_tok], normed[1])).astype(BF)
        apply_grad = (mm_tn(qall, delta_gate), mm_tn(qall, delta_up), mm_tn(odall, q_hidden))
        saved_f = [w.astype(F32) for w in saved]
        col_dot = [jnp.sum(saved_f[i] * apply_grad[i], axis=0, keepdims=True) for i in range(3)]
        cot = [
            apply_grad[i] * ratio[i] - saved_f[i] * (col_dot[i] * norm_init[i] / norm_saved[i] ** 3)
            for i in range(3)
        ]
        cb = [c.astype(BF) for c in cot]
        direct = [
            cot[i] + init[i].astype(F32) * (col_dot[i] / (norm_init[i] * norm_saved[i])) for i in range(3)
        ]

        kall = jnp.concatenate(ks, axis=0)
        vall = jnp.concatenate(vs, axis=0)
        k_gate = mm(kall, init[0])
        k_up = mm(kall, init[1])
        k_proj = mm(vall, init[2])
        k_act, k_slope, k_bend = silu_parts(k_gate)
        k_hidden = (k_act * k_up).astype(BF)
        rise_gate = (k_proj * k_up * k_slope).astype(BF)
        rise_up = (k_proj * k_act).astype(BF)
        back_gate = mm(kall, cb[0])
        back_up = mm(kall, cb[1])
        back_hidden = mm(vall, cb[2])
        back_proj = (back_gate * k_up * k_slope + back_up * k_act).astype(BF)
        back_kup = (back_gate * k_proj * k_slope + back_hidden * k_act).astype(BF)
        back_kgate = (
            back_gate * k_proj * k_up * k_bend + (back_up * k_proj + back_hidden * k_up) * k_slope
        ).astype(BF)
        gk = (
            mm_nt(rise_gate, cb[0]) + mm_nt(rise_up, cb[1]) + mm_nt(back_kgate, init[0]) + mm_nt(back_kup, init[1])
        ).astype(BF)
        gv = (mm_nt(k_hidden, cb[2]) + mm_nt(back_proj, init[2])).astype(BF)
        first = me < group
        inner = [mm_tn(kall, back_kgate), mm_tn(kall, back_kup), mm_tn(vall, back_proj)]
        inner = jnp.concatenate(
            [inner[i] + jnp.where(first, direct[i], 0.0) for i in range(3)], axis=1
        ).astype(BF)

        def home(x):
            return sum(
                send(x[d * own_tok : (d + 1) * own_tok], "seq", seq_n, d).astype(F32) for d in near
            )

        grad_q = home(gq).astype(BF)
        grad_k = home(gk).astype(BF)
        grad_v = (rates[:, None] * home(gv)).astype(BF)
        got = [
            send(lax.dynamic_slice_in_dim(inner, (me ^ d) * rows, rows, 0), "seq", seq_n, d) for d in every
        ]
        total = jnp.stack([sum(got[d].astype(F32) for d in every[e::group]) for e in near])
        cols = [lax.dynamic_index_in_dim(total, mine ^ j, 0, keepdims=False) for j in near]
        grads = [
            jnp.concatenate([c[:, i * slab : (i + 1) * slab] for c in cols], axis=1)[None] for i in range(3)
        ]
        return (grad_q[None], grad_k[None], grad_v[None], *grads)

    return local


def solution(mesh):
    seq_n = mesh.shape["seq"]
    head_n = mesh.shape["head"]
    group = min(4, seq_n)
    tok = P("head", "seq", None)
    return jax.shard_map(
        make_local(seq_n, head_n, group),
        mesh=mesh,
        in_specs=(tok, tok, tok, tok, P("head", "seq"), P("head", None), tok, tok, tok, tok, tok, tok),
        out_specs=(tok, tok, tok, tok, tok, tok),
        check_vma=False,
    )
```

time: 311 us -> 197 us (0.63)
  waiting for transfers between devices: 248 us -> 55.8 us
  starting transfers between devices: 0.16 us -> 79.5 us
  local copies, waits for them, and re-layouts: 14.4 us -> 33.3 us
  between operations: 14.2 us -> 1.5 us
  other arithmetic: 15.5 us -> 5.43 us
    psum x1 -> x0, waiting for transfers between devices: 104 us -> none  [local(): apply_full = lax.psum(apply_local, 'seq')]
    all_gather x2 -> x0, waiting for transfers between devices: 83.7 us -> none  [the longest x1 43.6 us: local(): lax.all_gather(saved_slab, 'seq', axis=0, tiled=True)]
    ppermute x0 -> x46, starting transfers between devices: none -> 79.5 us  [send(): return lax.ppermute(block, axis, [(i, i ^ dist) for i in range(size)])]
    unnamed x5 -> x0, waiting for transfers between devices: 60 us -> none
    ppermute x0 -> x46, waiting for transfers between devices: none -> 55.8 us  [send(): return lax.ppermute(block, axis, [(i, i ^ dist) for i in range(size)])]
    dynamic_update_slice x0 -> x8, local copies, waits for them, and re-layouts: none -> 24 us  [local(): wall = lax.dynamic_update_slice_in_dim(wall, wrecv[d], (me ^ d) * rows, 0)]
    unnamed x65 -> x39, local copies, waits for them, and re-layouts: 12.4 us -> 0.73 us
    another operation x0 -> x12, local copies, waits for them, and re-layouts: none -> 6.79 us  [the longest x8 6.25 us: local(): jnp.stack([w[0].reshape(rows, group, slab) for w in (gs, us, ds, gi, ui,...]
  transfers between devices with their start and end apart: 4 -> 46, of which waited for: 4 -> 10; matrix products, arithmetic and copies ran while one was open for 4% -> 26% of each run, Pallas kernels for 0% -> 0%
where the time goes in v1:
time: 197 us; the launch traced here: 196 us
  starting transfers between devices  79.5 us (40%)
  waiting for transfers between devices  55.8 us (28%)
  local copies, waits for them, and re-layouts  33.3 us (17%)
  matrix products  14.9 us (8%)
  blocking collectives  5.84 us (3%)
  other arithmetic  5.43 us (3%)
    ppermute x46, starting transfers between devices, send(): return lax.ppermute(block, axis, [(i, i ^ dist) for i in range(size)])  79.5 us
    ppermute x46, waiting for transfers between devices, send(): return lax.ppermute(block, axis, [(i, i ^ dist) for i in range(size)])  55.8 us
    dynamic_update_slice x8, local copies, waits for them, and re-layouts, local(): wall = lax.dynamic_update_slice_in_dim(wall, wrecv[d], (me ^ d) * rows, 0)  24 us
    dot_general x9, matrix products, mm(): return jnp.dot(left_op, right_op, preferred_element_type=F32)  8.77 us
    another operation x8, local copies, waits for them, and re-layouts, local(): jnp.stack([w[0].reshape(rows, group, slab) for w in (gs, us, ds, gi, ui,...  6.25 us
    psum x1, blocking collectives, local(): lax.psum(jnp.stack((jnp.sum(apply_out * apply_out, axis=1), jnp.sum(apply...  5.84 us
  transfers between devices with their start and end apart: 46, of which 10 were waited for; matrix products, arithmetic and copies ran while one was open for 26% of the time, Pallas kernels for 0%

profile of v1, /device:TPU:0, one launch (start us, length us, event | category | flops | bytes accessed | tf_op | source)
XLA Modules:
  0.0 196.2 jit_solution(8703160434139078998)
XLA Ops:
  0.6 3.0 %collective-permute-start = (bf16[128,256]{1,0:T(8,128)(2,1)}, bf16[128,256]{1,0:T(8,128)(2,1)S(1)}, u32[]{:S(2)}, u32[]{:S(2)}) collective-permute-start(bf16[128,256]{1,0:T(8,128)(2,1)} %bitcast.79), channel_id=1, source_target_pairs={{0,1},{1,0},{2,3},{3,2},{4,5},{5,4},{6,7},{7,6},{8,9},{9,8},{10,11... | collective-permute-start | bytes 196616 | tf_op jit(solution)/shard_map/ppermute | solution.py:39
  3.6 1.6 collective-permute-start.1
  5.2 3.0 %collective-permute-start.3 = (bf16[128,256]{1,0:T(8,128)(2,1)}, bf16[128,256]{1,0:T(8,128)(2,1)S(1)}, u32[]{:S(2)}, u32[]{:S(2)}) collective-permute-start(bf16[128,256]{1,0:T(8,128)(2,1)} %bitcast.82), channel_id=1, source_target_pairs={{0,4},{1,5},{2,6},{3,7},{4,0},{5,1},{6,2},{7,3},{8,12},{9,13},{10,... | collective-permute-start | bytes 196616 | tf_op jit(solution)/shard_map/ppermute | solution.py:39
  8.2 1.3 collective-permute-start.4
  9.5 0.9 stack_reshape_squeeze.18
  10.4 0.9 stack_reshape_squeeze.19
  11.4 0.9 stack_reshape_squeeze.20
  12.3 0.9 stack_reshape_squeeze.21
  13.2 0.9 stack_reshape_squeeze.22
  14.2 0.9 stack_reshape_squeeze.23
  16.2 1.0 dynamic-slice_bitcast_fusion
  17.4 2.1 %dynamic_update_slice.24 = bf16[256,1152]{0,1:T(8,128)(2,1)S(1)} dynamic-update-slice(bf16[256,1152]{0,1:T(8,128)(2,1)S(1)} %broadcast_in_dim.38, bf16[32,1152]{0,1:T(8,128)(2,1)S(1)} %get-tuple-element.29, s32[]{:T(128)S(6)} %select_n.67, s32[]{:T(128)} %constant.24.clone.1) | dynamic-update-slice | bytes 147460 | tf_op jit(solution)/shard_map/dynamic_update_slice | solution.py:67
  19.5 4.5 %collective-permute-start.5 = (bf16[128,256]{1,0:T(8,128)(2,1)S(1)}, bf16[128,256]{1,0:T(8,128)(2,1)S(1)}, u32[]{:S(2)}, u32[]{:S(2)}) collective-permute-start(bf16[128,256]{1,0:T(8,128)(2,1)S(1)} %bitcast.84), channel_id=1, source_target_pairs={{0,6},{1,7},{2,4},{3,5},{4,2},{5,3},{6,0},{7,1},{8,14},{9,15},{10,... | collective-permute-start | bytes 196616 | tf_op jit(solution)/shard_map/ppermute | solution.py:39
  24.4 0.8 collective-permute-start.10
  25.8 3.2 %collective-permute-start.11 = (bf16[32,1152]{0,1:T(8,128)(2,1)}, bf16[32,1152]{0,1:T(8,128)(2,1)S(1)}, u32[]{:S(2)}, u32[]{:S(2)}) collective-permute-start(bf16[32,1152]{0,1:T(8,128)(2,1)} %get-tuple-element.28), channel_id=1, source_target_pairs={{0,5},{1,4},{2,7},{3,6},{4,1},{5,0},{6,3},{7,2},{8,13},{9,12},{10,... | collective-permute-start | bytes 221192 | tf_op jit(solution)/shard_map/ppermute | solution.py:39
  29.1 10.5 %collective-permute-start.8 = (bf16[32,1152]{0,1:T(8,128)(2,1)}, bf16[32,1152]{0,1:T(8,128)(2,1)S(1)}, u32[]{:S(2)}, u32[]{:S(2)}) collective-permute-start(bf16[32,1152]{0,1:T(8,128)(2,1)} %get-tuple-element.27), channel_id=1, source_target_pairs={{0,2},{1,3},{2,0},{3,1},{4,6},{5,7},{6,4},{7,5},{8,10},{9,11},{10,... | collective-permute-start | bytes 221192 | tf_op jit(solution)/shard_map/ppermute | solution.py:39
  39.6 1.1 collective-permute-start.12
  40.7 2.7 %collective-permute-start.9 = (bf16[32,1152]{0,1:T(8,128)(2,1)}, bf16[32,1152]{0,1:T(8,128)(2,1)}, u32[]{:S(2)}, u32[]{:S(2)}) collective-permute-start(bf16[32,1152]{0,1:T(8,128)(2,1)} %get-tuple-element.26), channel_id=1, source_target_pairs={{0,3},{1,2},{2,1},{3,0},{4,7},{5,6},{6,5},{7,4},{8,11},{9,10},{10,... | collective-permute-start | bytes 221192 | tf_op jit(solution)/shard_map/ppermute | solution.py:39
  43.3 25.3 %collective-permute-done.8 = bf16[32,1152]{0,1:T(8,128)(2,1)S(1)} collective-permute-done((bf16[32,1152]{0,1:T(8,128)(2,1)}, bf16[32,1152]{0,1:T(8,128)(2,1)S(1)}, u32[]{:S(2)}, u32[]{:S(2)}) %collective-permute-start.8) | collective-permute-done | bytes 73760 | tf_op jit(solution)/shard_map/ppermute | solution.py:39
  68.6 1.3 collective-permute-start.13
  70.0 3.3 %dynamic_update_slice.25 = bf16[256,1152]{0,1:T(8,128)(2,1)S(1)} dynamic-update-slice(bf16[256,1152]{0,1:T(8,128)(2,1)S(1)} %dynamic_update_slice.24, bf16[32,1152]{0,1:T(8,128)(2,1)S(1)} %collective-permute-done.7, s32[]{:T(128)S(6)} %select_n.69, s32[]{:T(128)} %constant.24.clone.1) | dynamic-update-slice | bytes 147460 | tf_op jit(solution)/shard_map/dynamic_update_slice | solution.py:67
  73.3 3.4 %dynamic_update_slice.26 = bf16[256,1152]{0,1:T(8,128)(2,1)S(1)} dynamic-update-slice(bf16[256,1152]{0,1:T(8,128)(2,1)S(1)} %dynamic_update_slice.25, bf16[32,1152]{0,1:T(8,128)(2,1)S(1)} %collective-permute-done.8, s32[]{:T(128)S(6)} %select_n.71, s32[]{:T(128)} %constant.24.clone.1) | dynamic-update-slice | bytes 147460 | tf_op jit(solution)/shard_map/dynamic_update_slice | solution.py:67
  76.8 4.6 %dynamic_update_slice.27 = bf16[256,1152]{0,1:T(8,128)(2,1)S(1)} dynamic-update-slice(bf16[256,1152]{0,1:T(8,128)(2,1)S(1)} %dynamic_update_slice.26, bf16[32,1152]{0,1:T(8,128)(2,1)} %collective-permute-done.9, s32[]{:T(128)S(6)} %select_n.73, s32[]{:T(128)} %constant.24.clone.1) | dynamic-update-slice | bytes 147460 | tf_op jit(solution)/shard_map/dynamic_update_slice | solution.py:67
  81.3 1.7 collective-permute-start.31
  83.1 1.7 dynamic_update_slice.28
  84.8 2.3 %collective-permute-start.30 = (bf16[128,256]{1,0:T(8,128)(2,1)}, bf16[128,256]{1,0:T(8,128)(2,1)S(1)}, u32[]{:S(2)}, u32[]{:S(2)}) collective-permute-start(bf16[128,256]{1,0:T(8,128)(2,1)} %bitcast.15), channel_id=1, source_target_pairs={{0,1},{1,0},{2,3},{3,2},{4,5},{5,4},{6,7},{7,6},{8,9},{9,8},{10,11... | collective-permute-start | bytes 196616 | tf_op jit(solution)/shard_map/ppermute | solution.py:39
  87.0 2.9 %dynamic_update_slice.29 = bf16[256,1152]{0,1:T(8,128)(2,1)S(1)} dynamic-update-slice(bf16[256,1152]{0,1:T(8,128)(2,1)S(1)} %dynamic_update_slice.28, bf16[32,1152]{0,1:T(8,128)(2,1)S(1)} %collective-permute-done.11, s32[]{:T(128)S(6)} %select_n.75, s32[]{:T(128)} %constant.24.clone.1) | dynamic-update-slice | bytes 147460 | tf_op jit(solution)/shard_map/dynamic_update_slice | solution.py:67
  90.0 0.9 collective-permute-start.29
  91.0 2.9 %dynamic_update_slice.30 = bf16[256,1152]{0,1:T(8,128)(2,1)S(1)} dynamic-update-slice(bf16[256,1152]{0,1:T(8,128)(2,1)S(1)} %dynamic_update_slice.29, bf16[32,1152]{0,1:T(8,128)(2,1)S(1)} %collective-permute-done.12, s32[]{:T(128)S(6)} %select_n.76, s32[]{:T(128)} %constant.24.clone.1) | dynamic-update-slice | bytes 147460 | tf_op jit(solution)/shard_map/dynamic_update_slice | solution.py:67
  94.0 3.0 %dynamic_update_slice.31 = bf16[256,1152]{0,1:T(8,128)(2,1)S(1)} dynamic-update-slice(bf16[256,1152]{0,1:T(8,128)(2,1)S(1)} %dynamic_update_slice.30, bf16[32,1152]{0,1:T(8,128)(2,1)S(1)} %collective-permute-done.13, s32[]{:T(128)S(6)} %select_n.77, s32[]{:T(128)} %constant.24.clone.1) | dynamic-update-slice | bytes 147460 | tf_op jit(solution)/shard_map/dynamic_update_slice | solution.py:67
  97.7 1.3 multiply_convert_fusion.2
  99.3 0.9 collective-permute-start.16
  100.2 3.2 %collective-permute-start.15 = (bf16[128,256]{0,1:T(8,128)(2,1)S(1)}, bf16[128,256]{0,1:T(8,128)(2,1)S(1)}, u32[]{:S(2)}, u32[]{:S(2)}) collective-permute-start(bf16[128,256]{0,1:T(8,128)(2,1)S(1)} %get-tuple-element.55), channel_id=1, source_target_pairs={{0,2},{1,3},{2,0},{3,1},{4,6},{5,7},{6,4},{7,5},{8,10},{9,11},{10,... | collective-permute-start | bytes 196616 | tf_op jit(solution)/shard_map/ppermute | solution.py:39
  103.5 1.8 fusion.56
  105.3 1.9 fusion.59
  107.1 2.0 %collective-permute-start.27 = (bf16[128,256]{1,0:T(8,128)(2,1)S(1)}, bf16[128,256]{1,0:T(8,128)(2,1)S(1)}, u32[]{:S(2)}, u32[]{:S(2)}) collective-permute-start(bf16[128,256]{1,0:T(8,128)(2,1)S(1)} %fusion.42), channel_id=1, source_target_pairs={{0,1},{1,0},{2,3},{3,2},{4,5},{5,4},{6,7},{7,6},{8,9},{9,8},{10,11... | collective-permute-start | bytes 196616 | tf_op jit(solution)/shard_map/ppermute | solution.py:39
  109.3 5.8 %psum.7 = f32[2,128]{1,0:T(2,128)S(1)} all-reduce(f32[2,128]{1,0:T(2,128)S(1)} %pad_maximum_fusion.4), channel_id=1, replica_groups=mesh['head'=4,'seq'=8] {'head'}, use_global_device_ids=true, to_apply=%region_8.9 | all-reduce | flops 256 | bytes 2048 | tf_op jit(solution)/shard_map/psum | solution.py:87
  115.9 1.2 collective-permute-start.18
  117.1 2.0 %collective-permute-start.19 = (bf16[128,256]{0,1:T(8,128)(2,1)S(1)}, bf16[128,256]{0,1:T(8,128)(2,1)S(1)}, u32[]{:S(2)}, u32[]{:S(2)}) collective-permute-start(bf16[128,256]{0,1:T(8,128)(2,1)S(1)} %get-tuple-element.18), channel_id=1, source_target_pairs={{0,3},{1,2},{2,1},{3,0},{4,7},{5,6},{6,5},{7,4},{8,11},{9,10},{10,... | collective-permute-start | bytes 196616 | tf_op jit(solution)/shard_map/ppermute | solution.py:39
  119.2 2.8 %collective-permute-start.20 = (bf16[128,256]{0,1:T(8,128)(2,1)S(1)}, bf16[128,256]{0,1:T(8,128)(2,1)S(1)}, u32[]{:S(2)}, u32[]{:S(2)}) collective-permute-start(bf16[128,256]{0,1:T(8,128)(2,1)S(1)} %get-tuple-element.18), channel_id=1, source_target_pairs={{0,4},{1,5},{2,6},{3,7},{4,0},{5,1},{6,2},{7,3},{8,12},{9,13},{10,... | collective-permute-start | bytes 196616 | tf_op jit(solution)/shard_map/ppermute | solution.py:39
  122.6 4.3 %collective-permute-start.22 = (bf16[128,256]{0,1:T(8,128)(2,1)S(1)}, bf16[128,256]{0,1:T(8,128)(2,1)S(1)}, u32[]{:S(2)}, u32[]{:S(2)}) collective-permute-start(bf16[128,256]{0,1:T(8,128)(2,1)S(1)} %get-tuple-element.18), channel_id=1, source_target_pairs={{0,6},{1,7},{2,4},{3,5},{4,2},{5,3},{6,0},{7,1},{8,14},{9,15},{10,... | collective-permute-start | bytes 196616 | tf_op jit(solution)/shard_map/ppermute | solution.py:39
  127.2 4.8 %collective-permute-done.21 = bf16[128,256]{0,1:T(8,128)(2,1)S(1)} collective-permute-done((bf16[128,256]{0,1:T(8,128)(2,1)S(1)}, bf16[128,256]{0,1:T(8,128)(2,1)S(1)}, u32[]{:S(2)}, u32[]{:S(2)}) %collective-permute-start.21) | collective-permute-done | bytes 65568 | tf_op jit(solution)/shard_map/ppermute | solution.py:39
  132.0 2.1 %collective-permute-done.23 = bf16[128,256]{0,1:T(8,128)(2,1)S(1)} collective-permute-done((bf16[128,256]{0,1:T(8,128)(2,1)S(1)}, bf16[128,256]{0,1:T(8,128)(2,1)S(1)}, u32[]{:S(2)}, u32[]{:S(2)}) %collective-permute-start.23) | collective-permute-done | bytes 65568 | tf_op jit(solution)/shard_map/ppermute | solution.py:39
  136.0 1.7 collective-permute-start.26
  137.8 1.7 collective-permute-start.24
  140.9 1.1 fusion.81
  142.3 1.4 add_convert_fusion
  145.3 1.1 fusion.5
  146.4 1.1 fusion.4
  147.9 2.1 %collective-permute-start.45 = (bf16[32,576]{0,1:T(8,128)(2,1)S(1)}, bf16[32,576]{0,1:T(8,128)(2,1)S(1)}, u32[]{:S(2)}, u32[]{:S(2)}) collective-permute-start(bf16[32,576]{0,1:T(8,128)(2,1)S(1)} %get-tuple-element.38), channel_id=1, source_target_pairs={{0,7},{1,6},{2,5},{3,4},{4,3},{5,2},{6,1},{7,0},{8,15},{9,14},{10,... | collective-permute-start | bytes 110600 | tf_op jit(solution)/shard_map/ppermute | solution.py:39
  150.0 1.9 collective-permute-start.44
  152.0 4.3 %collective-permute-done.45 = bf16[32,576]{0,1:T(8,128)(2,1)S(1)} collective-permute-done((bf16[32,576]{0,1:T(8,128)(2,1)S(1)}, bf16[32,576]{0,1:T(8,128)(2,1)S(1)}, u32[]{:S(2)}, u32[]{:S(2)}) %collective-permute-start.45) | collective-permute-done | bytes 36896 | tf_op jit(solution)/shard_map/ppermute | solution.py:39
  156.3 3.0 %collective-permute-start.43 = (bf16[32,576]{0,1:T(8,128)(2,1)S(1)}, bf16[32,576]{0,1:T(8,128)(2,1)S(1)}, u32[]{:S(2)}, u32[]{:S(2)}) collective-permute-start(bf16[32,576]{0,1:T(8,128)(2,1)S(1)} %get-tuple-element.40), channel_id=1, source_target_pairs={{0,6},{1,7},{2,4},{3,5},{4,2},{5,3},{6,0},{7,1},{8,14},{9,15},{10,... | collective-permute-start | bytes 110600 | tf_op jit(solution)/shard_map/ppermute | solution.py:39
  159.3 1.3 collective-permute-start.42
  160.7 3.6 %collective-permute-done.43 = bf16[32,576]{0,1:T(8,128)(2,1)S(1)} collective-permute-done((bf16[32,576]{0,1:T(8,128)(2,1)S(1)}, bf16[32,576]{0,1:T(8,128)(2,1)S(1)}, u32[]{:S(2)}, u32[]{:S(2)}) %collective-permute-start.43) | collective-permute-done | bytes 36896 | tf_op jit(solution)/shard_map/ppermute | solution.py:39
  164.3 5.2 %collective-permute-start.41 = (bf16[32,576]{0,1:T(8,128)(2,1)S(1)}, bf16[32,576]{0,1:T(8,128)(2,1)S(1)}, u32[]{:S(2)}, u32[]{:S(2)}) collective-permute-start(bf16[32,576]{0,1:T(8,128)(2,1)S(1)} %get-tuple-element.42), channel_id=1, source_target_pairs={{0,5},{1,4},{2,7},{3,6},{4,1},{5,0},{6,3},{7,2},{8,13},{9,12},{10,... | collective-permute-start | bytes 110600 | tf_op jit(solution)/shard_map/ppermute | solution.py:39
  169.9 6.7 %collective-permute-done.41 = bf16[32,576]{0,1:T(8,128)(2,1)S(1)} collective-permute-done((bf16[32,576]{0,1:T(8,128)(2,1)S(1)}, bf16[32,576]{0,1:T(8,128)(2,1)S(1)}, u32[]{:S(2)}, u32[]{:S(2)}) %collective-permute-start.41) | collective-permute-done | bytes 36896 | tf_op jit(solution)/shard_map/ppermute | solution.py:39
  177.1 7.2 %collective-permute-done.39 = bf16[32,576]{0,1:T(8,128)(2,1)S(1)} collective-permute-done((bf16[32,576]{0,1:T(8,128)(2,1)S(1)}, bf16[32,576]{0,1:T(8,128)(2,1)S(1)}, u32[]{:S(2)}, u32[]{:S(2)}) %collective-permute-start.39) | collective-permute-done | bytes 36896 | tf_op jit(solution)/shard_map/ppermute | solution.py:39
  184.9 0.7 maximum_bitcast_fusion
  185.6 0.7 maximum_bitcast_fusion.1
  186.3 0.7 maximum_bitcast_fusion.2
  187.1 1.9 collective-permute-start.33
  189.0 1.6 collective-permute-start.38
  191.2 1.9 collective-permute-start.36
  (151 shorter events, 15.9 us)
Async XLA Ops:
  0.6 18.9 %collective-permute-start = (bf16[128,256]{1,0:T(8,128)(2,1)}, bf16[128,256]{1,0:T(8,128)(2,1)S(1)}, u32[]{:S(2)}, u32[]{:S(2)}) collective-permute-start(bf16[128,256]{1,0:T(8,128)(2,1)} %bitcast.79), channel_id=1, source_target_pairs={{0,1},{1,0},{2,3},{3,2},{4,5},{5,4},{6,7},{7,6},{8,9},{9,8},{10,11... | collective-permute-start | bytes 196616 | tf_op jit(solution)/shard_map/ppermute | solution.py:39
  3.6 20.4 %collective-permute-start.1 = (bf16[128,256]{1,0:T(8,128)(2,1)}, bf16[128,256]{1,0:T(8,128)(2,1)S(1)}, u32[]{:S(2)}, u32[]{:S(2)}) collective-permute-start(bf16[128,256]{1,0:T(8,128)(2,1)} %bitcast.80), channel_id=1, source_target_pairs={{0,2},{1,3},{2,0},{3,1},{4,6},{5,7},{6,4},{7,5},{8,10},{9,11},{10,... | collective-permute-start | bytes 196616 | tf_op jit(solution)/shard_map/ppermute | solution.py:39
  5.2 19.2 %collective-permute-start.2 = (bf16[128,256]{1,0:T(8,128)(2,1)}, bf16[128,256]{1,0:T(8,128)(2,1)S(1)}, u32[]{:S(2)}, u32[]{:S(2)}) collective-permute-start(bf16[128,256]{1,0:T(8,128)(2,1)} %bitcast.81), channel_id=1, source_target_pairs={{0,3},{1,2},{2,1},{3,0},{4,7},{5,6},{6,5},{7,4},{8,11},{9,10},{10,... | collective-permute-start | bytes 196616 | tf_op jit(solution)/shard_map/ppermute | solution.py:39
  5.2 20.0 %collective-permute-start.3 = (bf16[128,256]{1,0:T(8,128)(2,1)}, bf16[128,256]{1,0:T(8,128)(2,1)S(1)}, u32[]{:S(2)}, u32[]{:S(2)}) collective-permute-start(bf16[128,256]{1,0:T(8,128)(2,1)} %bitcast.82), channel_id=1, source_target_pairs={{0,4},{1,5},{2,6},{3,7},{4,0},{5,1},{6,2},{7,3},{8,12},{9,13},{10,... | collective-permute-start | bytes 196616 | tf_op jit(solution)/shard_map/ppermute | solution.py:39
  8.2 17.6 %collective-permute-start.4 = (bf16[128,256]{1,0:T(8,128)(2,1)}, bf16[128,256]{1,0:T(8,128)(2,1)S(1)}, u32[]{:S(2)}, u32[]{:S(2)}) collective-permute-start(bf16[128,256]{1,0:T(8,128)(2,1)} %bitcast.83), channel_id=1, source_target_pairs={{0,5},{1,4},{2,7},{3,6},{4,1},{5,0},{6,3},{7,2},{8,13},{9,12},{10,... | collective-permute-start | bytes 196616 | tf_op jit(solution)/shard_map/ppermute | solution.py:39
  14.1 1.9 copy-start
  14.1 1.9 copy-start.4
  16.1 1.0 copy-start.2
  16.2 1.0 copy-start.1
  19.5 9.5 %collective-permute-start.5 = (bf16[128,256]{1,0:T(8,128)(2,1)S(1)}, bf16[128,256]{1,0:T(8,128)(2,1)S(1)}, u32[]{:S(2)}, u32[]{:S(2)}) collective-permute-start(bf16[128,256]{1,0:T(8,128)(2,1)S(1)} %bitcast.84), channel_id=1, source_target_pairs={{0,6},{1,7},{2,4},{3,5},{4,2},{5,3},{6,0},{7,1},{8,14},{9,15},{10,... | collective-permute-start | bytes 196616 | tf_op jit(solution)/shard_map/ppermute | solution.py:39
  24.1 15.5 %collective-permute-start.6 = (bf16[128,256]{1,0:T(8,128)(2,1)S(1)}, bf16[128,256]{1,0:T(8,128)(2,1)S(1)}, u32[]{:S(2)}, u32[]{:S(2)}) collective-permute-start(bf16[128,256]{1,0:T(8,128)(2,1)S(1)} %bitcast.85), channel_id=1, source_target_pairs={{0,7},{1,6},{2,5},{3,4},{4,3},{5,2},{6,1},{7,0},{8,15},{9,14},{10,... | collective-permute-start | bytes 196616 | tf_op jit(solution)/shard_map/ppermute | solution.py:39
  24.4 56.9 %collective-permute-start.10 = (bf16[32,1152]{0,1:T(8,128)(2,1)S(1)}, bf16[32,1152]{0,1:T(8,128)(2,1)S(1)}, u32[]{:S(2)}, u32[]{:S(2)}) collective-permute-start(bf16[32,1152]{0,1:T(8,128)(2,1)S(1)} %get-tuple-element.29), channel_id=1, source_target_pairs={{0,4},{1,5},{2,6},{3,7},{4,0},{5,1},{6,2},{7,3},{8,12},{9,13},{10,... | collective-permute-start | bytes 221192 | tf_op jit(solution)/shard_map/ppermute | solution.py:39
  25.2 15.4 %collective-permute-start.7 = (bf16[32,1152]{0,1:T(8,128)(2,1)}, bf16[32,1152]{0,1:T(8,128)(2,1)S(1)}, u32[]{:S(2)}, u32[]{:S(2)}) collective-permute-start(bf16[32,1152]{0,1:T(8,128)(2,1)} %get-tuple-element.28), channel_id=1, source_target_pairs={{0,1},{1,0},{2,3},{3,2},{4,5},{5,4},{6,7},{7,6},{8,9},{9,8},{10,11... | collective-permute-start | bytes 221192 | tf_op jit(solution)/shard_map/ppermute | solution.py:39
  25.8 58.9 %collective-permute-start.11 = (bf16[32,1152]{0,1:T(8,128)(2,1)}, bf16[32,1152]{0,1:T(8,128)(2,1)S(1)}, u32[]{:S(2)}, u32[]{:S(2)}) collective-permute-start(bf16[32,1152]{0,1:T(8,128)(2,1)} %get-tuple-element.28), channel_id=1, source_target_pairs={{0,5},{1,4},{2,7},{3,6},{4,1},{5,0},{6,3},{7,2},{8,13},{9,12},{10,... | collective-permute-start | bytes 221192 | tf_op jit(solution)/shard_map/ppermute | solution.py:39
  29.1 39.6 %collective-permute-start.8 = (bf16[32,1152]{0,1:T(8,128)(2,1)}, bf16[32,1152]{0,1:T(8,128)(2,1)S(1)}, u32[]{:S(2)}, u32[]{:S(2)}) collective-permute-start(bf16[32,1152]{0,1:T(8,128)(2,1)} %get-tuple-element.27), channel_id=1, source_target_pairs={{0,2},{1,3},{2,0},{3,1},{4,6},{5,7},{6,4},{7,5},{8,10},{9,11},{10,... | collective-permute-start | bytes 221192 | tf_op jit(solution)/shard_map/ppermute | solution.py:39
  39.6 50.4 %collective-permute-start.12 = (bf16[32,1152]{0,1:T(8,128)(2,1)}, bf16[32,1152]{0,1:T(8,128)(2,1)S(1)}, u32[]{:S(2)}, u32[]{:S(2)}) collective-permute-start(bf16[32,1152]{0,1:T(8,128)(2,1)} %get-tuple-element.27), channel_id=1, source_target_pairs={{0,6},{1,7},{2,4},{3,5},{4,2},{5,3},{6,0},{7,1},{8,14},{9,15},{10,... | collective-permute-start | bytes 221192 | tf_op jit(solution)/shard_map/ppermute | solution.py:39
  40.7 36.0 %collective-permute-start.9 = (bf16[32,1152]{0,1:T(8,128)(2,1)}, bf16[32,1152]{0,1:T(8,128)(2,1)}, u32[]{:S(2)}, u32[]{:S(2)}) collective-permute-start(bf16[32,1152]{0,1:T(8,128)(2,1)} %get-tuple-element.26), channel_id=1, source_target_pairs={{0,3},{1,2},{2,1},{3,0},{4,7},{5,6},{6,5},{7,4},{8,11},{9,10},{10,... | collective-permute-start | bytes 221192 | tf_op jit(solution)/shard_map/ppermute | solution.py:39
  68.6 25.3 %collective-permute-start.13 = (bf16[32,1152]{0,1:T(8,128)(2,1)}, bf16[32,1152]{0,1:T(8,128)(2,1)S(1)}, u32[]{:S(2)}, u32[]{:S(2)}) collective-permute-start(bf16[32,1152]{0,1:T(8,128)(2,1)} %get-tuple-element.26), channel_id=1, source_target_pairs={{0,7},{1,6},{2,5},{3,4},{4,3},{5,2},{6,1},{7,0},{8,15},{9,14},{10,... | collective-permute-start | bytes 221192 | tf_op jit(solution)/shard_map/ppermute | solution.py:39
  76.7 22.7 %collective-permute-start.32 = (bf16[128,256]{1,0:T(8,128)(2,1)}, bf16[128,256]{1,0:T(8,128)(2,1)S(1)}, u32[]{:S(2)}, u32[]{:S(2)}) collective-permute-start(bf16[128,256]{1,0:T(8,128)(2,1)} %bitcast.15), channel_id=1, source_target_pairs={{0,3},{1,2},{2,1},{3,0},{4,7},{5,6},{6,5},{7,4},{8,11},{9,10},{10,... | collective-permute-start | bytes 196616 | tf_op jit(solution)/shard_map/ppermute | solution.py:39
  81.3 18.9 %collective-permute-start.31 = (bf16[128,256]{1,0:T(8,128)(2,1)}, bf16[128,256]{1,0:T(8,128)(2,1)S(1)}, u32[]{:S(2)}, u32[]{:S(2)}) collective-permute-start(bf16[128,256]{1,0:T(8,128)(2,1)} %bitcast.15), channel_id=1, source_target_pairs={{0,2},{1,3},{2,0},{3,1},{4,6},{5,7},{6,4},{7,5},{8,10},{9,11},{10,... | collective-permute-start | bytes 196616 | tf_op jit(solution)/shard_map/ppermute | solution.py:39
  84.8 18.7 %collective-permute-start.30 = (bf16[128,256]{1,0:T(8,128)(2,1)}, bf16[128,256]{1,0:T(8,128)(2,1)S(1)}, u32[]{:S(2)}, u32[]{:S(2)}) collective-permute-start(bf16[128,256]{1,0:T(8,128)(2,1)} %bitcast.15), channel_id=1, source_target_pairs={{0,1},{1,0},{2,3},{3,2},{4,5},{5,4},{6,7},{7,6},{8,9},{9,8},{10,11... | collective-permute-start | bytes 196616 | tf_op jit(solution)/shard_map/ppermute | solution.py:39
  90.0 25.7 %collective-permute-start.29 = (bf16[128,256]{1,0:T(8,128)(2,1)S(1)}, bf16[128,256]{1,0:T(8,128)(2,1)S(1)}, u32[]{:S(2)}, u32[]{:S(2)}) collective-permute-start(bf16[128,256]{1,0:T(8,128)(2,1)S(1)} %fusion.42), channel_id=1, source_target_pairs={{0,3},{1,2},{2,1},{3,0},{4,7},{5,6},{6,5},{7,4},{8,11},{9,10},{10,... | collective-permute-start | bytes 196616 | tf_op jit(solution)/shard_map/ppermute | solution.py:39
  93.9 21.7 %collective-permute-start.28 = (bf16[128,256]{1,0:T(8,128)(2,1)S(1)}, bf16[128,256]{1,0:T(8,128)(2,1)S(1)}, u32[]{:S(2)}, u32[]{:S(2)}) collective-permute-start(bf16[128,256]{1,0:T(8,128)(2,1)S(1)} %fusion.42), channel_id=1, source_target_pairs={{0,2},{1,3},{2,0},{3,1},{4,6},{5,7},{6,4},{7,5},{8,10},{9,11},{10,... | collective-permute-start | bytes 196616 | tf_op jit(solution)/shard_map/ppermute | solution.py:39
  99.3 9.9 %copy-start.3 = (f32[1,256]{1,0:T(1,128)S(1)}, f32[1,256]{1,0:T(1,128)}, u32[]{:S(2)}) copy-start(f32[1,256]{1,0:T(1,128)} %param.17) | copy-start | bytes 3076
  99.3 7.8 %collective-permute-start.16 = (bf16[128,256]{0,1:T(8,128)(2,1)S(1)}, bf16[128,256]{0,1:T(8,128)(2,1)S(1)}, u32[]{:S(2)}, u32[]{:S(2)}) collective-permute-start(bf16[128,256]{0,1:T(8,128)(2,1)S(1)} %get-tuple-element.54), channel_id=1, source_target_pairs={{0,3},{1,2},{2,1},{3,0},{4,7},{5,6},{6,5},{7,4},{8,11},{9,10},{10,... | collective-permute-start | bytes 196616 | tf_op jit(solution)/shard_map/ppermute | solution.py:39
  100.2 8.9 %collective-permute-start.15 = (bf16[128,256]{0,1:T(8,128)(2,1)S(1)}, bf16[128,256]{0,1:T(8,128)(2,1)S(1)}, u32[]{:S(2)}, u32[]{:S(2)}) collective-permute-start(bf16[128,256]{0,1:T(8,128)(2,1)S(1)} %get-tuple-element.55), channel_id=1, source_target_pairs={{0,2},{1,3},{2,0},{3,1},{4,6},{5,7},{6,4},{7,5},{8,10},{9,11},{10,... | collective-permute-start | bytes 196616 | tf_op jit(solution)/shard_map/ppermute | solution.py:39
  103.5 5.7 %collective-permute-start.14 = (bf16[128,256]{0,1:T(8,128)(2,1)S(1)}, bf16[128,256]{0,1:T(8,128)(2,1)S(1)}, u32[]{:S(2)}, u32[]{:S(2)}) collective-permute-start(bf16[128,256]{0,1:T(8,128)(2,1)S(1)} %get-tuple-element.53), channel_id=1, source_target_pairs={{0,1},{1,0},{2,3},{3,2},{4,5},{5,4},{6,7},{7,6},{8,9},{9,8},{10,11... | collective-permute-start | bytes 196616 | tf_op jit(solution)/shard_map/ppermute | solution.py:39
  107.1 8.5 %collective-permute-start.27 = (bf16[128,256]{1,0:T(8,128)(2,1)S(1)}, bf16[128,256]{1,0:T(8,128)(2,1)S(1)}, u32[]{:S(2)}, u32[]{:S(2)}) collective-permute-start(bf16[128,256]{1,0:T(8,128)(2,1)S(1)} %fusion.42), channel_id=1, source_target_pairs={{0,1},{1,0},{2,3},{3,2},{4,5},{5,4},{6,7},{7,6},{8,9},{9,8},{10,11... | collective-permute-start | bytes 196616 | tf_op jit(solution)/shard_map/ppermute | solution.py:39
  115.3 7.3 %collective-permute-start.17 = (bf16[128,256]{0,1:T(8,128)(2,1)S(1)}, bf16[128,256]{0,1:T(8,128)(2,1)S(1)}, u32[]{:S(2)}, u32[]{:S(2)}) collective-permute-start(bf16[128,256]{0,1:T(8,128)(2,1)S(1)} %get-tuple-element.18), channel_id=1, source_target_pairs={{0,1},{1,0},{2,3},{3,2},{4,5},{5,4},{6,7},{7,6},{8,9},{9,8},{10,11... | collective-permute-start | bytes 196616 | tf_op jit(solution)/shard_map/ppermute | solution.py:39
  115.7 26.3 %copy-start.5 = (bf16[128,256]{1,0:T(8,128)(2,1)}, bf16[128,256]{1,0:T(8,128)(2,1)S(1)}, u32[]{:S(2)}) copy-start(bf16[128,256]{1,0:T(8,128)(2,1)S(1)} %collective-permute-done.27) | copy-start | bytes 196612
  115.9 18.5 %copy-start.9 = (f32[1024,192]{0,1:T(8,128)S(1)}, f32[1024,192]{0,1:T(8,128)}, u32[]{:S(2)}) copy-start(f32[1024,192]{0,1:T(8,128)} %get-tuple-element.75) | copy-start | bytes 2359300
  115.9 11.0 %collective-permute-start.18 = (bf16[128,256]{0,1:T(8,128)(2,1)S(1)}, bf16[128,256]{0,1:T(8,128)(2,1)S(1)}, u32[]{:S(2)}, u32[]{:S(2)}) collective-permute-start(bf16[128,256]{0,1:T(8,128)(2,1)S(1)} %get-tuple-element.18), channel_id=1, source_target_pairs={{0,2},{1,3},{2,0},{3,1},{4,6},{5,7},{6,4},{7,5},{8,10},{9,11},{10,... | collective-permute-start | bytes 196616 | tf_op jit(solution)/shard_map/ppermute | solution.py:39
  117.1 9.9 %collective-permute-start.19 = (bf16[128,256]{0,1:T(8,128)(2,1)S(1)}, bf16[128,256]{0,1:T(8,128)(2,1)S(1)}, u32[]{:S(2)}, u32[]{:S(2)}) collective-permute-start(bf16[128,256]{0,1:T(8,128)(2,1)S(1)} %get-tuple-element.18), channel_id=1, source_target_pairs={{0,3},{1,2},{2,1},{3,0},{4,7},{5,6},{6,5},{7,4},{8,11},{9,10},{10,... | collective-permute-start | bytes 196616 | tf_op jit(solution)/shard_map/ppermute | solution.py:39
  119.2 7.9 %collective-permute-start.20 = (bf16[128,256]{0,1:T(8,128)(2,1)S(1)}, bf16[128,256]{0,1:T(8,128)(2,1)S(1)}, u32[]{:S(2)}, u32[]{:S(2)}) collective-permute-start(bf16[128,256]{0,1:T(8,128)(2,1)S(1)} %get-tuple-element.18), channel_id=1, source_target_pairs={{0,4},{1,5},{2,6},{3,7},{4,0},{5,1},{6,2},{7,3},{8,12},{9,13},{10,... | collective-permute-start | bytes 196616 | tf_op jit(solution)/shard_map/ppermute | solution.py:39
  122.0 10.0 %collective-permute-start.21 = (bf16[128,256]{0,1:T(8,128)(2,1)S(1)}, bf16[128,256]{0,1:T(8,128)(2,1)S(1)}, u32[]{:S(2)}, u32[]{:S(2)}) collective-permute-start(bf16[128,256]{0,1:T(8,128)(2,1)S(1)} %get-tuple-element.18), channel_id=1, source_target_pairs={{0,5},{1,4},{2,7},{3,6},{4,1},{5,0},{6,3},{7,2},{8,13},{9,12},{10,... | collective-permute-start | bytes 196616 | tf_op jit(solution)/shard_map/ppermute | solution.py:39
  122.6 9.3 %collective-permute-start.22 = (bf16[128,256]{0,1:T(8,128)(2,1)S(1)}, bf16[128,256]{0,1:T(8,128)(2,1)S(1)}, u32[]{:S(2)}, u32[]{:S(2)}) collective-permute-start(bf16[128,256]{0,1:T(8,128)(2,1)S(1)} %get-tuple-element.18), channel_id=1, source_target_pairs={{0,6},{1,7},{2,4},{3,5},{4,2},{5,3},{6,0},{7,1},{8,14},{9,15},{10,... | collective-permute-start | bytes 196616 | tf_op jit(solution)/shard_map/ppermute | solution.py:39
  127.0 7.1 %collective-permute-start.23 = (bf16[128,256]{0,1:T(8,128)(2,1)S(1)}, bf16[128,256]{0,1:T(8,128)(2,1)S(1)}, u32[]{:S(2)}, u32[]{:S(2)}) collective-permute-start(bf16[128,256]{0,1:T(8,128)(2,1)S(1)} %get-tuple-element.18), channel_id=1, source_target_pairs={{0,7},{1,6},{2,5},{3,4},{4,3},{5,2},{6,1},{7,0},{8,15},{9,14},{10,... | collective-permute-start | bytes 196616 | tf_op jit(solution)/shard_map/ppermute | solution.py:39
  136.0 51.1 %collective-permute-start.26 = (bf16[128,256]{1,0:T(8,128)(2,1)S(1)}, bf16[128,256]{1,0:T(8,128)(2,1)S(1)}, u32[]{:S(2)}, u32[]{:S(2)}) collective-permute-start(bf16[128,256]{1,0:T(8,128)(2,1)S(1)} %get-tuple-element.51), channel_id=1, source_target_pairs={{0,3},{1,2},{2,1},{3,0},{4,7},{5,6},{6,5},{7,4},{8,11},{9,10},{10,... | collective-permute-start | bytes 196616 | tf_op jit(solution)/shard_map/ppermute | solution.py:39
  137.7 51.3 %collective-permute-start.25 = (bf16[128,256]{1,0:T(8,128)(2,1)S(1)}, bf16[128,256]{1,0:T(8,128)(2,1)S(1)}, u32[]{:S(2)}, u32[]{:S(2)}) collective-permute-start(bf16[128,256]{1,0:T(8,128)(2,1)S(1)} %get-tuple-element.52), channel_id=1, source_target_pairs={{0,2},{1,3},{2,0},{3,1},{4,6},{5,7},{6,4},{7,5},{8,10},{9,11},{10,... | collective-permute-start | bytes 196616 | tf_op jit(solution)/shard_map/ppermute | solution.py:39
  137.8 2.4 %copy-start.7 = (f32[512,192]{0,1:T(8,128)S(1)}, f32[512,192]{0,1:T(8,128)}, u32[]{:S(2)}) copy-start(f32[512,192]{0,1:T(8,128)} %fusion.59) | copy-start | bytes 1179652
  137.8 2.4 %copy-start.8 = (f32[512,192]{0,1:T(8,128)S(1)}, f32[512,192]{0,1:T(8,128)}, u32[]{:S(2)}) copy-start(f32[512,192]{0,1:T(8,128)} %fusion.56) | copy-start | bytes 1179652
  137.8 52.8 %collective-permute-start.24 = (bf16[128,256]{1,0:T(8,128)(2,1)S(1)}, bf16[128,256]{1,0:T(8,128)(2,1)S(1)}, u32[]{:S(2)}, u32[]{:S(2)}) collective-permute-start(bf16[128,256]{1,0:T(8,128)(2,1)S(1)} %get-tuple-element.50), channel_id=1, source_target_pairs={{0,1},{1,0},{2,3},{3,2},{4,5},{5,4},{6,7},{7,6},{8,9},{9,8},{10,11... | collective-permute-start | bytes 196616 | tf_op jit(solution)/shard_map/ppermute | solution.py:39
  144.3 0.8 copy-start.6
  147.9 8.4 %collective-permute-start.45 = (bf16[32,576]{0,1:T(8,128)(2,1)S(1)}, bf16[32,576]{0,1:T(8,128)(2,1)S(1)}, u32[]{:S(2)}, u32[]{:S(2)}) collective-permute-start(bf16[32,576]{0,1:T(8,128)(2,1)S(1)} %get-tuple-element.38), channel_id=1, source_target_pairs={{0,7},{1,6},{2,5},{3,4},{4,3},{5,2},{6,1},{7,0},{8,15},{9,14},{10,... | collective-permute-start | bytes 110600 | tf_op jit(solution)/shard_map/ppermute | solution.py:39
  150.0 9.3 %collective-permute-start.44 = (bf16[32,576]{0,1:T(8,128)(2,1)S(1)}, bf16[32,576]{0,1:T(8,128)(2,1)S(1)}, u32[]{:S(2)}, u32[]{:S(2)}) collective-permute-start(bf16[32,576]{0,1:T(8,128)(2,1)S(1)} %get-tuple-element.39), channel_id=1, source_target_pairs={{0,3},{1,2},{2,1},{3,0},{4,7},{5,6},{6,5},{7,4},{8,11},{9,10},{10,... | collective-permute-start | bytes 110600 | tf_op jit(solution)/shard_map/ppermute | solution.py:39
  156.3 8.0 %collective-permute-start.43 = (bf16[32,576]{0,1:T(8,128)(2,1)S(1)}, bf16[32,576]{0,1:T(8,128)(2,1)S(1)}, u32[]{:S(2)}, u32[]{:S(2)}) collective-permute-start(bf16[32,576]{0,1:T(8,128)(2,1)S(1)} %get-tuple-element.40), channel_id=1, source_target_pairs={{0,6},{1,7},{2,4},{3,5},{4,2},{5,3},{6,0},{7,1},{8,14},{9,15},{10,... | collective-permute-start | bytes 110600 | tf_op jit(solution)/shard_map/ppermute | solution.py:39
  159.3 10.2 %collective-permute-start.42 = (bf16[32,576]{0,1:T(8,128)(2,1)S(1)}, bf16[32,576]{0,1:T(8,128)(2,1)S(1)}, u32[]{:S(2)}, u32[]{:S(2)}) collective-permute-start(bf16[32,576]{0,1:T(8,128)(2,1)S(1)} %get-tuple-element.41), channel_id=1, source_target_pairs={{0,2},{1,3},{2,0},{3,1},{4,6},{5,7},{6,4},{7,5},{8,10},{9,11},{10,... | collective-permute-start | bytes 110600 | tf_op jit(solution)/shard_map/ppermute | solution.py:39
  164.3 12.3 %collective-permute-start.41 = (bf16[32,576]{0,1:T(8,128)(2,1)S(1)}, bf16[32,576]{0,1:T(8,128)(2,1)S(1)}, u32[]{:S(2)}, u32[]{:S(2)}) collective-permute-start(bf16[32,576]{0,1:T(8,128)(2,1)S(1)} %get-tuple-element.42), channel_id=1, source_target_pairs={{0,5},{1,4},{2,7},{3,6},{4,1},{5,0},{6,3},{7,2},{8,13},{9,12},{10,... | collective-permute-start | bytes 110600 | tf_op jit(solution)/shard_map/ppermute | solution.py:39
  169.5 7.1 %collective-permute-start.40 = (bf16[32,576]{0,1:T(8,128)(2,1)S(1)}, bf16[32,576]{0,1:T(8,128)(2,1)S(1)}, u32[]{:S(2)}, u32[]{:S(2)}) collective-permute-start(bf16[32,576]{0,1:T(8,128)(2,1)S(1)} %get-tuple-element.43), channel_id=1, source_target_pairs={{0,1},{1,0},{2,3},{3,2},{4,5},{5,4},{6,7},{7,6},{8,9},{9,8},{10,11... | collective-permute-start | bytes 110600 | tf_op jit(solution)/shard_map/ppermute | solution.py:39
  176.6 14.7 %collective-permute-start.35 = (bf16[128,256]{1,0:T(8,128)(2,1)S(1)}, bf16[128,256]{1,0:T(8,128)(2,1)S(1)}, u32[]{:S(2)}, u32[]{:S(2)}) collective-permute-start(bf16[128,256]{1,0:T(8,128)(2,1)S(1)} %get-tuple-element.48), channel_id=1, source_target_pairs={{0,3},{1,2},{2,1},{3,0},{4,7},{5,6},{6,5},{7,4},{8,11},{9,10},{10,... | collective-permute-start | bytes 196616 | tf_op jit(solution)/shard_map/ppermute | solution.py:39
  176.6 7.6 %collective-permute-start.39 = (bf16[32,576]{0,1:T(8,128)(2,1)S(1)}, bf16[32,576]{0,1:T(8,128)(2,1)S(1)}, u32[]{:S(2)}, u32[]{:S(2)}) collective-permute-start(bf16[32,576]{0,1:T(8,128)(2,1)S(1)} %get-tuple-element.37), channel_id=1, source_target_pairs={{0,4},{1,5},{2,6},{3,7},{4,0},{5,1},{6,2},{7,3},{8,12},{9,13},{10,... | collective-permute-start | bytes 110600 | tf_op jit(solution)/shard_map/ppermute | solution.py:39
  184.2 8.9 %collective-permute-start.34 = (bf16[128,256]{1,0:T(8,128)(2,1)S(1)}, bf16[128,256]{1,0:T(8,128)(2,1)S(1)}, u32[]{:S(2)}, u32[]{:S(2)}) collective-permute-start(bf16[128,256]{1,0:T(8,128)(2,1)S(1)} %get-tuple-element.49), channel_id=1, source_target_pairs={{0,2},{1,3},{2,0},{3,1},{4,6},{5,7},{6,4},{7,5},{8,10},{9,11},{10,... | collective-permute-start | bytes 196616 | tf_op jit(solution)/shard_map/ppermute | solution.py:39
  187.1 6.1 %collective-permute-start.33 = (bf16[128,256]{1,0:T(8,128)(2,1)S(1)}, bf16[128,256]{1,0:T(8,128)(2,1)S(1)}, u32[]{:S(2)}, u32[]{:S(2)}) collective-permute-start(bf16[128,256]{1,0:T(8,128)(2,1)S(1)} %get-tuple-element.47), channel_id=1, source_target_pairs={{0,1},{1,0},{2,3},{3,2},{4,5},{5,4},{6,7},{7,6},{8,9},{9,8},{10,11... | collective-permute-start | bytes 196616 | tf_op jit(solution)/shard_map/ppermute | solution.py:39
  189.0 5.2 %collective-permute-start.38 = (bf16[128,256]{1,0:T(8,128)(2,1)S(1)}, bf16[128,256]{1,0:T(8,128)(2,1)S(1)}, u32[]{:S(2)}, u32[]{:S(2)}) collective-permute-start(bf16[128,256]{1,0:T(8,128)(2,1)S(1)} %get-tuple-element.45), channel_id=1, source_target_pairs={{0,3},{1,2},{2,1},{3,0},{4,7},{5,6},{6,5},{7,4},{8,11},{9,10},{10,... | collective-permute-start | bytes 196616 | tf_op jit(solution)/shard_map/ppermute | solution.py:39
  190.6 4.3 %collective-permute-start.37 = (bf16[128,256]{1,0:T(8,128)(2,1)S(1)}, bf16[128,256]{1,0:T(8,128)(2,1)S(1)}, u32[]{:S(2)}, u32[]{:S(2)}) collective-permute-start(bf16[128,256]{1,0:T(8,128)(2,1)S(1)} %get-tuple-element.46), channel_id=1, source_target_pairs={{0,2},{1,3},{2,0},{3,1},{4,6},{5,7},{6,4},{7,5},{8,10},{9,11},{10,... | collective-permute-start | bytes 196616 | tf_op jit(solution)/shard_map/ppermute | solution.py:39
  191.2 4.3 %collective-permute-start.36 = (bf16[128,256]{1,0:T(8,128)(2,1)S(1)}, bf16[128,256]{1,0:T(8,128)(2,1)S(1)}, u32[]{:S(2)}, u32[]{:S(2)}) collective-permute-start(bf16[128,256]{1,0:T(8,128)(2,1)S(1)} %get-tuple-element.44), channel_id=1, source_target_pairs={{0,1},{1,0},{2,3},{3,2},{4,5},{5,4},{6,7},{7,6},{8,9},{9,8},{10,11... | collective-permute-start | bytes 196616 | tf_op jit(solution)/shard_map/ppermute | solution.py:39

commit v2 on v1

--- a/solution.py
+++ b/solution.py
@@ -33,10 +33,12 @@
     return jnp.sqrt(jnp.sum(jnp.square(weight.astype(F32)), axis=0, keepdims=True) + EPS_COL)
 
 
-def send(block, axis, size, dist):
-    if dist == 0:
-        return block
-    return lax.ppermute(block, axis, [(i, i ^ dist) for i in range(size)])
+def swap(blocks, groups=None):
+    return lax.all_to_all(blocks, "seq", 0, 0, axis_index_groups=groups, tiled=True)
+
+
+def share(block, size, groups=None):
+    return swap(jnp.broadcast_to(block[None], (size,) + block.shape), groups)
 
 
 def make_local(seq_n, head_n, group):
@@ -48,23 +50,23 @@
         feat = q.shape[1]
         width = head_n * feat
         me = lax.axis_index("seq")
-        mine = lax.rem(me, group)
         near = range(group)
-        every = range(seq_n)
+        tok_groups = seq_n // group
+        groups = [[t * group + j for j in near] for t in range(tok_groups)]
+        own_tok = q.shape[0]
+        near_tok = group * own_tok
+        start = lax.div(me, group) * near_tok
+
+        def mine(x):
+            return lax.dynamic_slice_in_dim(x, start, near_tok, 0)
 
         sv = (rates[:, None] * v.astype(F32)).astype(BF)
         packed = jnp.stack([w[0].reshape(rows, group, slab) for w in (gs, us, ds, gi, ui, di)], axis=2)
         packed = packed.reshape(rows, group, 6 * slab).transpose(1, 0, 2)
-        wsend = [lax.dynamic_index_in_dim(packed, mine ^ d, 0, keepdims=False) for d in near]
-        wrecv = [send(wsend[d % group], "seq", seq_n, d) for d in every]
-        qs = [send(q, "seq", seq_n, d) for d in near]
-        ks = [send(k, "seq", seq_n, d) for d in near]
-        vs = [send(sv, "seq", seq_n, d) for d in near]
-        qs += [send(q, "seq", seq_n, d) for d in every[group:]]
-
-        wall = jnp.zeros((seq_n * rows, 6 * slab), BF)
-        for d in every:
-            wall = lax.dynamic_update_slice_in_dim(wall, wrecv[d], (me ^ d) * rows, 0)
+        wall = swap(jnp.tile(packed, (tok_groups, 1, 1))).reshape(seq_n * rows, 6 * slab)
+        qall = share(q, seq_n).reshape(seq_n * own_tok, feat)
+        kvall = share(jnp.concatenate((k, sv), axis=1), group, groups).reshape(near_tok, 2 * feat)
+        kall, vall = kvall[:, :feat], kvall[:, feat:]
         saved = [wall[:, i * slab : (i + 1) * slab] for i in range(3)]
         init = [wall[:, (i + 3) * slab : (i + 4) * slab] for i in range(3)]
         norm_init = [column_norm(w) for w in init]
@@ -72,16 +74,12 @@
         ratio = [norm_init[i] / norm_saved[i] for i in range(3)]
         normed = [(saved[i].astype(F32) * ratio[i]).astype(BF) for i in range(3)]
 
-        qall = jnp.concatenate(qs, axis=0)
         q_gate = mm(qall, normed[0])
         q_up = mm(qall, normed[1])
         act, slope, _ = silu_parts(q_gate)
         q_hidden = (act * q_up).astype(BF)
-        own_tok = q.shape[0]
-        near_tok = group * own_tok
-        part = mm_nt(q_hidden[:near_tok], normed[2]).astype(BF)
-        parts = [send(part[d * own_tok : (d + 1) * own_tok], "seq", seq_n, d) for d in near]
-        apply_out = sum(p.astype(F32) for p in parts)
+        part = mm_nt(mine(q_hidden), normed[2]).astype(BF)
+        apply_out = jnp.sum(swap(part.reshape(group, own_tok, feat), groups).astype(F32), axis=0)
 
         gg = gains * og.astype(F32)
         sums = lax.psum(
@@ -90,12 +88,12 @@
         root = jnp.sqrt(sums[0] / width + EPS_ROOT)[:, None]
         gain_dot = (sums[1] / width)[:, None]
         out_delta = (gg / root - apply_out * gain_dot / root**3).astype(BF)
-        odall = jnp.concatenate([send(out_delta, "seq", seq_n, d) for d in every], axis=0)
+        odall = share(out_delta, seq_n).reshape(seq_n * own_tok, feat)
 
         delta_hidden = mm(odall, normed[2])
         delta_gate = (delta_hidden * q_up * slope).astype(BF)
         delta_up = (delta_hidden * act).astype(BF)
-        gq = (mm_nt(delta_gate[:near_tok], normed[0]) + mm_nt(delta_up[:near_tok], normed[1])).astype(BF)
+        gq = (mm_nt(mine(delta_gate), normed[0]) + mm_nt(mine(delta_up), normed[1])).astype(BF)
         apply_grad = (mm_tn(qall, delta_gate), mm_tn(qall, delta_up), mm_tn(odall, q_hidden))
         saved_f = [w.astype(F32) for w in saved]
         col_dot = [jnp.sum(saved_f[i] * apply_grad[i], axis=0, keepdims=True) for i in range(3)]
@@ -108,8 +106,6 @@
             cot[i] + init[i].astype(F32) * (col_dot[i] / (norm_init[i] * norm_saved[i])) for i in range(3)
         ]
 
-        kall = jnp.concatenate(ks, axis=0)
-        vall = jnp.concatenate(vs, axis=0)
         k_gate = mm(kall, init[0])
         k_up = mm(kall, init[1])
         k_proj = mm(vall, init[2])
@@ -135,22 +131,14 @@
             [inner[i] + jnp.where(first, direct[i], 0.0) for i in range(3)], axis=1
         ).astype(BF)
 
-        def home(x):
-            return sum(
-                send(x[d * own_tok : (d + 1) * own_tok], "seq", seq_n, d).astype(F32) for d in near
-            )
-
-        grad_q = home(gq).astype(BF)
-        grad_k = home(gk).astype(BF)
-        grad_v = (rates[:, None] * home(gv)).astype(BF)
-        got = [
-            send(lax.dynamic_slice_in_dim(inner, (me ^ d) * rows, rows, 0), "seq", seq_n, d) for d in every
-        ]
-        total = jnp.stack([sum(got[d].astype(F32) for d in every[e::group]) for e in near])
-        cols = [lax.dynamic_index_in_dim(total, mine ^ j, 0, keepdims=False) for j in near]
-        grads = [
-            jnp.concatenate([c[:, i * slab : (i + 1) * slab] for c in cols], axis=1)[None] for i in range(3)
-        ]
+        tokens = jnp.concatenate((gq, gk, gv), axis=1).reshape(group, own_tok, 3 * feat)
+        tokens = jnp.sum(swap(tokens, groups).astype(F32), axis=0)
+        grad_q = tokens[:, :feat].astype(BF)
+        grad_k = tokens[:, feat : 2 * feat].astype(BF)
+        grad_v = (rates[:, None] * tokens[:, 2 * feat :]).astype(BF)
+        got = swap(inner.reshape(seq_n, rows, 3 * slab)).reshape(tok_groups, group, rows, 3, slab)
+        got = jnp.sum(got.astype(F32), axis=0).transpose(2, 1, 0, 3).reshape(3, rows, hidden)
+        grads = [got[i][None] for i in range(3)]
         return (grad_q[None], grad_k[None], grad_v[None], *grads)
 
     return local

time: 197 us -> 134 us (0.68)
  starting transfers between devices: 79.5 us -> 21.8 us
  blocking collectives: 5.84 us -> 29.3 us
  waiting for transfers between devices: 55.8 us -> 39.3 us
  local copies, waits for them, and re-layouts: 33.3 us -> 21.3 us
    ppermute x46 -> x0, starting transfers between devices: 79.5 us -> none  [send(): return lax.ppermute(block, axis, [(i, i ^ dist) for i in range(size)])]
    ppermute x46 -> x0, waiting for transfers between devices: 55.8 us -> none  [send(): return lax.ppermute(block, axis, [(i, i ^ dist) for i in range(size)])]
    all_to_all x0 -> x6, waiting for transfers between devices: none -> 39.3 us  [swap(): lax.all_to_all(blocks, 'seq', 0, 0, axis_index_groups=groups, tiled=True)]
    dynamic_update_slice x8 -> x0, local copies, waits for them, and re-layouts: 24 us -> none  [local(): wall = lax.dynamic_update_slice_in_dim(wall, wrecv[d], (me ^ d) * rows, 0)]
    all_to_all x0 -> x1, blocking collectives: none -> 23.6 us  [swap(): lax.all_to_all(blocks, 'seq', 0, 0, axis_index_groups=groups, tiled=True)]
    all_to_all x0 -> x6, starting transfers between devices: none -> 21.8 us  [swap(): lax.all_to_all(blocks, 'seq', 0, 0, axis_index_groups=groups, tiled=True)]
    unnamed x39 -> x94, local copies, waits for them, and re-layouts: 0.73 us -> 8.9 us
    broadcast_in_dim x1 -> x4, local copies, waits for them, and re-layouts: 0.04 us -> 2.52 us  [the longest x3 2.51 us: share(): return swap(jnp.broadcast_to(block[None], (size,) + block.shape), groups)]
  transfers between devices with their start and end apart: 46 -> 6, of which waited for: 10 -> 6; matrix products, arithmetic and copies ran while one was open for 26% -> 9% of each run, Pallas kernels for 0% -> 0%
where the time goes in v2:
time: 134 us; the launch traced here: 133 us
  waiting for transfers between devices  39.3 us (29%)
  blocking collectives  29.3 us (22%)
  starting transfers between devices  21.8 us (16%)
  local copies, waits for them, and re-layouts  21.3 us (16%)
  matrix products  14.9 us (11%)
  other arithmetic  4.87 us (4%)
  between operations  1.46 us (1%)
    all_to_all x6, waiting for transfers between devices, swap(): lax.all_to_all(blocks, 'seq', 0, 0, axis_index_groups=groups, tiled=True)  39.3 us
    all_to_all x1, blocking collectives, swap(): lax.all_to_all(blocks, 'seq', 0, 0, axis_index_groups=groups, tiled=True)  23.6 us
    all_to_all x6, starting transfers between devices, swap(): lax.all_to_all(blocks, 'seq', 0, 0, axis_index_groups=groups, tiled=True)  21.8 us
    unnamed x94, local copies, waits for them, and re-layouts  8.9 us
    dot_general x9, matrix products, mm(): return jnp.dot(left_op, right_op, preferred_element_type=F32)  8.16 us
    another operation x13, local copies, waits for them, and re-layouts, local(): jnp.stack([w[0].reshape(rows, group, slab) for w in (gs, us, ds, gi, ui,...  5.77 us
    psum x1, blocking collectives, local(): lax.psum(jnp.stack((jnp.sum(apply_out * apply_out, axis=1), jnp.sum(apply...  5.67 us
    dot_general x9, matrix products, mm_nt(): lax.dot_general(left_op, right_op, (((1,), (1,)), ((), ())), preferred_el...  4.28 us
  transfers between devices with their start and end apart: 6, of which 6 were waited for; matrix products, arithmetic and copies ran while one was open for 9% of the time, Pallas kernels for 0%

profile of v2, /device:TPU:0, one launch (start us, length us, event | category | flops | bytes accessed | tf_op | source)
XLA Modules:
  0.0 132.9 jit_solution(14818114537793588409)
XLA Ops:
  0.7 0.9 stack_reshape_squeeze.18
  1.7 0.9 stack_reshape_squeeze.19
  2.7 0.9 stack_reshape_squeeze.20
  3.8 0.9 stack_reshape_squeeze.21
  5.3 1.2 stack.12
  6.5 0.4 reshape.261
  7.0 23.6 %all_to_all.35 = bf16[8,32,1152]{2,1,0:T(8,128)(2,1)S(1)} all-to-all(bf16[8,32,1152]{2,1,0:T(8,128)(2,1)S(1)} %bitcast.105), channel_id=1, replica_groups=mesh['head'=4,'seq'=8] {'seq'}, dimensions={0} | all-to-all | bytes 1179648 | tf_op jit(solution)/shard_map/all_to_all | solution.py:37
  30.6 0.8 broadcast_in_dim.22
  31.4 3.5 %all-to-all-start.1 = ((bf16[8,128,256]{2,1,0:T(8,128)(2,1)}), bf16[8,128,256]{2,1,0:T(8,128)(2,1)S(1)}, u32[]{:S(2)}, u32[]{:S(2)}) async-start(bf16[8,128,256]{2,1,0:T(8,128)(2,1)} %broadcast_in_dim.22), calls=%async_computation.1 | async-start | bytes 1048576 | tf_op jit(solution)/shard_map/all_to_all | solution.py:37
  35.9 12.8 %all-to-all-done.1 = bf16[8,128,256]{2,1,0:T(8,128)(2,1)S(1)} async-done(((bf16[8,128,256]{2,1,0:T(8,128)(2,1)}), bf16[8,128,256]{2,1,0:T(8,128)(2,1)S(1)}, u32[]{:S(2)}, u32[]{:S(2)}) %all-to-all-start.1) | async-done | bytes 524320 | tf_op jit(solution)/shard_map/all_to_all | solution.py:37
  48.7 0.3 convolution_bitcast_fusion.1
  49.2 0.6 copy-done.25
  49.9 1.3 multiply_convert_fusion.2
  51.4 1.0 convolution_convert_fusion
  52.4 3.4 %all-to-all-start.2 = ((bf16[4,128,256]{2,1,0:T(8,128)(2,1)}), bf16[4,128,256]{2,1,0:T(8,128)(2,1)S(1)}, u32[]{:S(2)}, u32[]{:S(2)}) async-start(bf16[4,128,256]{2,1,0:T(8,128)(2,1)} %bitcast.8), calls=%async_computation.2 | async-start | bytes 524288 | tf_op jit(solution)/shard_map/all_to_all | solution.py:37
  56.3 4.9 %all-to-all-done.2 = bf16[4,128,256]{2,1,0:T(8,128)(2,1)S(1)} async-done(((bf16[4,128,256]{2,1,0:T(8,128)(2,1)}), bf16[4,128,256]{2,1,0:T(8,128)(2,1)S(1)}, u32[]{:S(2)}, u32[]{:S(2)}) %all-to-all-start.2) | async-done | bytes 262176 | tf_op jit(solution)/shard_map/all_to_all | solution.py:37
  61.2 0.8 broadcast_in_dim.26
  62.0 3.5 %all-to-all-start.4 = ((bf16[4,128,512]{2,1,0:T(8,128)(2,1)}), bf16[4,128,512]{2,1,0:T(8,128)(2,1)S(1)}, u32[]{:S(2)}, u32[]{:S(2)}) async-start(bf16[4,128,512]{2,1,0:T(8,128)(2,1)} %broadcast_in_dim.26), calls=%async_computation.4 | async-start | bytes 1048576 | tf_op jit(solution)/shard_map/all_to_all | solution.py:37
  65.7 5.7 %psum.7 = f32[2,128]{1,0:T(2,128)S(1)} all-reduce(f32[2,128]{1,0:T(2,128)S(1)} %pad_maximum_fusion.2), channel_id=1, replica_groups=mesh['head'=4,'seq'=8] {'head'}, use_global_device_ids=true, to_apply=%region_9.0 | all-reduce | flops 256 | bytes 2048 | tf_op jit(solution)/shard_map/psum | solution.py:85
  71.5 0.5 all-to-all-done.4
  72.0 0.8 broadcast_in_dim.25
  72.9 4.2 %all-to-all-start.3 = ((bf16[8,128,256]{2,1,0:T(8,128)(2,1)}), bf16[8,128,256]{2,1,0:T(8,128)(2,1)S(1)}, u32[]{:S(2)}, u32[]{:S(2)}) async-start(bf16[8,128,256]{2,1,0:T(8,128)(2,1)} %broadcast_in_dim.25), calls=%async_computation.3 | async-start | bytes 1048576 | tf_op jit(solution)/shard_map/all_to_all | solution.py:37
  77.1 1.1 fusion.63
  78.1 1.1 fusion.17
  79.2 1.0 fusion.65
  80.2 11.1 %all-to-all-done.3 = bf16[8,128,256]{2,1,0:T(8,128)(2,1)S(1)} async-done(((bf16[8,128,256]{2,1,0:T(8,128)(2,1)}), bf16[8,128,256]{2,1,0:T(8,128)(2,1)S(1)}, u32[]{:S(2)}, u32[]{:S(2)}) %all-to-all-start.3) | async-done | bytes 524320 | tf_op jit(solution)/shard_map/all_to_all | solution.py:37
  91.3 0.4 fusion.38
  91.7 0.8 copy-done.40
  92.5 1.7 %multiply_convert_fusion.1 = (bf16[1024,192]{0,1:T(8,128)(2,1)S(1)}, bf16[1024,192]{0,1:T(8,128)(2,1)S(1)}) fusion(f32[1024,192]{0,1:T(8,128)} %copy-done, f32[1024,192]{0,1:T(8,128)S(1)} %copy-done.40, bf16[1024,256]{1,0:T(8,128)(2,1)S(1)} %bitcast.107, bf16[256,192]{0,1:T(8,128)(2,1)S(1)} %copy.102, f32[192]{0:T(256)S(1)} %rsqrt_multiply_fusion), kind=kOutput, calls=%fused_computation.23 | convolution fusion | flops 103366656 | bytes 2982656 | tf_op jit(solution)/shard_map/dot_general | solution.py:21
  94.1 0.4 fusion.30
  94.5 0.3 fusion.42
  94.9 0.6 multiply_divide_fusion
  95.5 0.4 fusion.34
  95.8 0.6 multiply_divide_fusion.1
  96.4 0.6 copy-done.35
  97.2 0.2 fusion.59
  98.4 1.2 fusion.40
  99.6 1.3 add_convert_fusion.1
  100.8 0.7 copy-done.16
  101.9 0.9 fusion.4
  103.3 0.9 pad_maximum_fusion
  104.1 3.7 %all-to-all-start.6 = ((bf16[8,32,576]{2,1,0:T(8,128)(2,1)}), bf16[8,32,576]{2,1,0:T(8,128)(2,1)S(1)}, u32[]{:S(2)}, u32[]{:S(2)}) async-start(bf16[8,32,576]{2,1,0:T(8,128)(2,1)} %pad_maximum_fusion), calls=%async_computation.6 | async-start | bytes 655360 | tf_op jit(solution)/shard_map/all_to_all | solution.py:37
  107.9 0.3 fusion
  108.3 0.7 copy-done.39
  108.9 0.3 convolution_add_fusion.1
  109.3 0.6 copy-done.17
  109.9 0.3 convolution_add_fusion.4
  110.1 0.6 copy-done.15
  111.0 0.3 fusion.82
  111.3 0.5 copy-done.4
  111.8 0.3 fusion.1
  112.2 1.0 copy_bitcast_fusion
  113.2 5.0 %all-to-all-done.6 = bf16[8,32,576]{2,1,0:T(8,128)(2,1)S(1)} async-done(((bf16[8,32,576]{2,1,0:T(8,128)(2,1)}), bf16[8,32,576]{2,1,0:T(8,128)(2,1)S(1)}, u32[]{:S(2)}, u32[]{:S(2)}) %all-to-all-start.6) | async-done | bytes 294944 | tf_op jit(solution)/shard_map/all_to_all | solution.py:37
  118.2 3.5 %all-to-all-start.5 = ((bf16[4,128,768]{1,2,0:T(8,128)(2,1)}), bf16[4,128,768]{1,2,0:T(8,128)(2,1)S(1)}, u32[]{:S(2)}, u32[]{:S(2)}) async-start(bf16[4,128,768]{1,2,0:T(8,128)(2,1)} %copy_bitcast_fusion), calls=%async_computation.5 | async-start | bytes 1572864 | tf_op jit(solution)/shard_map/all_to_all | solution.py:37
  121.7 0.5 reshape.270
  122.2 0.5 reduce_sum.142
  122.7 0.3 fusion.93
  123.1 0.8 slice.73
  124.0 0.8 slice.75
  124.8 0.8 slice.77
  125.6 5.0 %all-to-all-done.5 = bf16[4,128,768]{1,2,0:T(8,128)(2,1)S(1)} async-done(((bf16[4,128,768]{1,2,0:T(8,128)(2,1)}), bf16[4,128,768]{1,2,0:T(8,128)(2,1)S(1)}, u32[]{:S(2)}, u32[]{:S(2)}) %all-to-all-start.5) | async-done | bytes 786464 | tf_op jit(solution)/shard_map/all_to_all | solution.py:37
  130.7 0.7 copy.94
  131.5 0.7 copy.95
  132.2 0.7 copy.96
  (125 shorter events, 5.4 us)
Async XLA Ops:
  0.6 4.2 %copy-start.23 = (bf16[1,32,768]{2,1,0:T(8,128)(2,1)S(1)}, bf16[1,32,768]{2,1,0:T(8,128)(2,1)}, u32[]{:S(2)}) copy-start(bf16[1,32,768]{2,1,0:T(8,128)(2,1)} %param.19) | copy-start | bytes 147460
  0.6 4.4 %copy-start.24 = (bf16[1,32,768]{2,1,0:T(8,128)(2,1)S(1)}, bf16[1,32,768]{2,1,0:T(8,128)(2,1)}, u32[]{:S(2)}) copy-start(bf16[1,32,768]{2,1,0:T(8,128)(2,1)} %param.20) | copy-start | bytes 147460
  6.9 23.7 %copy-start.20 = (bf16[1,128,256]{2,1,0:T(8,128)(2,1)S(1)}, bf16[1,128,256]{2,1,0:T(8,128)(2,1)}, u32[]{:S(2)}) copy-start(bf16[1,128,256]{2,1,0:T(8,128)(2,1)} %param.12) | copy-start | bytes 196612
  31.4 17.3 %all-to-all-start.1 = ((bf16[8,128,256]{2,1,0:T(8,128)(2,1)}), bf16[8,128,256]{2,1,0:T(8,128)(2,1)S(1)}, u32[]{:S(2)}, u32[]{:S(2)}) async-start(bf16[8,128,256]{2,1,0:T(8,128)(2,1)} %broadcast_in_dim.22), calls=%async_computation.1 | async-start | bytes 1048576 | tf_op jit(solution)/shard_map/all_to_all | solution.py:37
  49.1 2.1 %copy-start = (f32[1024,192]{0,1:T(8,128)}, f32[1024,192]{0,1:T(8,128)S(1)}, u32[]{:S(2)}) copy-start(f32[1024,192]{0,1:T(8,128)S(1)} %convolution_bitcast_fusion.1) | copy-start | bytes 2359300
  49.2 0.7 copy-start.25
  49.2 0.7 copy-start.27
  51.2 4.9 %copy-start.7 = (bf16[1024,192]{0,1:T(8,128)(2,1)}, bf16[1024,192]{0,1:T(8,128)(2,1)S(1)}, u32[]{:S(2)}) copy-start(bf16[1024,192]{0,1:T(8,128)(2,1)S(1)} %get-tuple-element.44) | copy-start | bytes 1179652
  51.2 4.6 %copy-start.21 = (bf16[1,128,256]{2,1,0:T(8,128)(2,1)S(1)}, bf16[1,128,256]{2,1,0:T(8,128)(2,1)}, u32[]{:S(2)}) copy-start(bf16[1,128,256]{2,1,0:T(8,128)(2,1)} %param.14) | copy-start | bytes 196612
  51.2 4.8 %copy-start.22 = (bf16[1,128,256]{2,1,0:T(8,128)(2,1)S(1)}, bf16[1,128,256]{2,1,0:T(8,128)(2,1)}, u32[]{:S(2)}) copy-start(bf16[1,128,256]{2,1,0:T(8,128)(2,1)} %param.13) | copy-start | bytes 196612
  51.2 4.9 %copy-start.36 = (f32[1,128]{1,0:T(1,128)S(1)}, f32[1,128]{1,0:T(1,128)}, u32[]{:S(2)}) copy-start(f32[1,128]{1,0:T(1,128)} %param.16) | copy-start | bytes 1540
  51.4 40.3 %copy-start.30 = (f32[192]{0:T(256)}, f32[192]{0:T(256)S(1)}, u32[]{:S(2)}) copy-start(f32[192]{0:T(256)S(1)} %rsqrt_multiply_fusion) | copy-start | bytes 2308
  52.4 8.8 %all-to-all-start.2 = ((bf16[4,128,256]{2,1,0:T(8,128)(2,1)}), bf16[4,128,256]{2,1,0:T(8,128)(2,1)S(1)}, u32[]{:S(2)}, u32[]{:S(2)}) async-start(bf16[4,128,256]{2,1,0:T(8,128)(2,1)} %bitcast.8), calls=%async_computation.2 | async-start | bytes 524288 | tf_op jit(solution)/shard_map/all_to_all | solution.py:37
  56.3 9.3 %copy-start.11 = (bf16[1,128,256]{2,1,0:T(8,128)(2,1)S(1)}, bf16[1,128,256]{2,1,0:T(8,128)(2,1)}, u32[]{:S(2)}) copy-start(bf16[1,128,256]{2,1,0:T(8,128)(2,1)} %param.15) | copy-start | bytes 196612
  56.3 9.3 %copy-start.29 = (f32[1,256]{1,0:T(1,128)S(1)}, f32[1,256]{1,0:T(1,128)}, u32[]{:S(2)}) copy-start(f32[1,256]{1,0:T(1,128)} %param.17) | copy-start | bytes 3076
  62.0 10.0 %all-to-all-start.4 = ((bf16[4,128,512]{2,1,0:T(8,128)(2,1)}), bf16[4,128,512]{2,1,0:T(8,128)(2,1)S(1)}, u32[]{:S(2)}, u32[]{:S(2)}) async-start(bf16[4,128,512]{2,1,0:T(8,128)(2,1)} %broadcast_in_dim.26), calls=%async_computation.4 | async-start | bytes 1048576 | tf_op jit(solution)/shard_map/all_to_all | solution.py:37
  72.9 18.5 %all-to-all-start.3 = ((bf16[8,128,256]{2,1,0:T(8,128)(2,1)}), bf16[8,128,256]{2,1,0:T(8,128)(2,1)S(1)}, u32[]{:S(2)}, u32[]{:S(2)}) async-start(bf16[8,128,256]{2,1,0:T(8,128)(2,1)} %broadcast_in_dim.25), calls=%async_computation.3 | async-start | bytes 1048576 | tf_op jit(solution)/shard_map/all_to_all | solution.py:37
  77.1 14.3 %copy-start.8 = (bf16[1024,192]{0,1:T(8,128)(2,1)S(1)}, bf16[1024,192]{0,1:T(8,128)(2,1)}, u32[]{:S(2)}) copy-start(bf16[1024,192]{0,1:T(8,128)(2,1)} %copy-done.7) | copy-start | bytes 1179652
  91.3 1.1 copy-start.40
  94.5 1.3 copy-start.26
  94.5 1.3 copy-start.28
  95.5 2.3 %copy-start.33 = (f32[192]{0:T(256)}, f32[192]{0:T(256)S(1)}, u32[]{:S(2)}) copy-start(f32[192]{0:T(256)S(1)} %get-tuple-element.43) | copy-start | bytes 2308
  96.4 0.6 copy-start.35
  97.1 0.8 copy-start.9
  97.1 0.7 copy-start.31
  97.1 1.0 copy-start.1
  97.1 1.1 copy-start.3
  97.2 1.3 copy-start.5
  98.4 1.2 copy-start.18
  100.8 0.7 copy-start.16
  100.8 1.0 copy-start.14
  101.5 1.4 %copy-start.12 = (bf16[512,192]{0,1:T(8,128)(2,1)S(1)}, bf16[512,192]{0,1:T(8,128)(2,1)}, u32[]{:S(2)}) copy-start(bf16[512,192]{0,1:T(8,128)(2,1)} %get-tuple-element.24) | copy-start | bytes 589828
  101.5 1.4 %copy-start.32 = (f32[192]{0:T(256)S(1)}, f32[192]{0:T(256)}, u32[]{:S(2)}) copy-start(f32[192]{0:T(256)} %copy-done.30) | copy-start | bytes 2308
  101.5 1.4 %copy-start.34 = (f32[192]{0:T(256)S(1)}, f32[192]{0:T(256)}, u32[]{:S(2)}) copy-start(f32[192]{0:T(256)} %copy-done.33) | copy-start | bytes 2308
  101.7 1.2 copy-start.38
  104.1 4.1 %copy-start.2 = (f32[512,192]{0,1:T(8,128)S(1)}, f32[512,192]{0,1:T(8,128)}, u32[]{:S(2)}) copy-start(f32[512,192]{0,1:T(8,128)} %fusion.63) | copy-start | bytes 1179652
  104.1 4.1 %copy-start.6 = (f32[512,192]{0,1:T(8,128)S(1)}, f32[512,192]{0,1:T(8,128)}, u32[]{:S(2)}) copy-start(f32[512,192]{0,1:T(8,128)} %fusion.17) | copy-start | bytes 1179652
  104.1 4.1 %copy-start.10 = (bf16[256,192]{0,1:T(8,128)(2,1)S(1)}, bf16[256,192]{0,1:T(8,128)(2,1)}, u32[]{:S(2)}) copy-start(bf16[256,192]{0,1:T(8,128)(2,1)} %copy-done.9) | copy-start | bytes 294916
  104.1 14.1 %all-to-all-start.6 = ((bf16[8,32,576]{2,1,0:T(8,128)(2,1)}), bf16[8,32,576]{2,1,0:T(8,128)(2,1)S(1)}, u32[]{:S(2)}, u32[]{:S(2)}) async-start(bf16[8,32,576]{2,1,0:T(8,128)(2,1)} %pad_maximum_fusion), calls=%async_computation.6 | async-start | bytes 655360 | tf_op jit(solution)/shard_map/all_to_all | solution.py:37
  107.9 1.0 copy-start.39
  108.9 0.9 copy-start.17
  109.9 0.9 copy-start.15
  109.9 1.2 copy-start.13
  110.8 1.0 copy-start.4
  110.8 1.0 copy-start.19
  118.2 12.3 %all-to-all-start.5 = ((bf16[4,128,768]{1,2,0:T(8,128)(2,1)}), bf16[4,128,768]{1,2,0:T(8,128)(2,1)S(1)}, u32[]{:S(2)}, u32[]{:S(2)}) async-start(bf16[4,128,768]{1,2,0:T(8,128)(2,1)} %copy_bitcast_fusion), calls=%async_computation.5 | async-start | bytes 1572864 | tf_op jit(solution)/shard_map/all_to_all | solution.py:37
  124.8 5.9 %copy-start.37 = (f32[1,128]{1,0:T(1,128)S(1)}, f32[1,128]{1,0:T(1,128)}, u32[]{:S(2)}) copy-start(f32[1,128]{1,0:T(1,128)} %param.16) | copy-start | bytes 1540
